TPU v7x, 32 devices: a whole 2x2x4 slice. The times are simulated.
32 devices in a mesh: blk: 16 (over z, x, core), dp: 2 (over y).
Axes of the slice: x: 2, y: 2, z: 4, core: 2. Of those that a mesh axis runs over, the one named last changes fastest.
Arguments:
- hidden_in: bfloat16 [4, 4096, 512], P('dp', 'blk'), may hold values from -6 to 6
- item_lengths: int32 [4, 64], P('dp'), may hold values from 0 to 4096, as said below
- live_mask: int32 [4, 4096], P('dp', 'blk'), may hold values 0 or 1
- cotangent: bfloat16 [4, 4096, 512], P('dp', 'blk'), may hold values from -6 to 6
- query_weight: bfloat16 [512, 384], replicated, may hold values from -0.125 to 0.125
- key_weight: bfloat16 [512, 384], replicated, may hold values from -0.125 to 0.125
- value_weight: bfloat16 [512, 384], replicated, may hold values from -0.25 to 0.25
- output_weight: bfloat16 [384, 512], replicated, may hold values from -1.25 to 1.25
- bucket_bias_table: float32 [32, 6], replicated, may hold values from -4 to 4
- norm_attention: float32 [512], replicated, may hold values from 0.5 to 1.5
- norm_feed: float32 [512], replicated, may hold values from 0.5 to 1.5
- gate_weight: bfloat16 [512, 1024], replicated, may hold values from -0.25 to 0.25
- up_weight: bfloat16 [512, 1024], replicated, may hold values from -0.25 to 0.25
- down_weight: bfloat16 [1024, 512], replicated, may hold values from -0.1875 to 0.1875
Outputs:
- output: bfloat16 [4, 4096, 512], P('dp', 'blk')
- input_gradient: bfloat16 [4, 4096, 512], P('dp', 'blk')
- query_weight_gradient: float32 [512, 384], replicated
- key_weight_gradient: float32 [512, 384], replicated
- value_weight_gradient: float32 [512, 384], replicated
- output_weight_gradient: float32 [384, 512], replicated
- bias_table_gradient: float32 [32, 6], replicated
- norm_attention_gradient: float32 [512], replicated
- norm_feed_gradient: float32 [512], replicated
- gate_weight_grad_sum: float32 [512, 1024], replicated
- up_weight_gradient: float32 [512, 1024], replicated
- down_weight_gradient: float32 [1024, 512], replicated
Inputs may be any that keep to these rules, and one draw needn't show every extreme that they name: `item_lengths`: row s lists the lengths of the items of stream s in order from the stream's first position, and sums to 4096; items may be empty. The first item of every row holds more than 3840 positions; one row, drawn from the seed, is a single item of 4096 positions followed by empty items.
All inputs are finite; a program needn't handle non-finite values. No bound on the sum of `live_mask` on one device may be relied on, other than what follows from the above.
Results may differ from a plain program's by a relative error of at most 0.03.
Values may be sent and summed in bfloat16 or wider, within the bound.
No kernel may reach another device: no remote copies, remote signals or barrier semaphores. Data moves between devices by JAX's collectives and lax.ppermute only.
A program may use at most 128 MiB of HBM per device.

v0:
```python
import jax
import jax.numpy as jnp
from jax import lax
from jax.sharding import PartitionSpec as P

HEADS = 6
HD = 64
BUCKETS = 32
MAXDIST = 128


EPSILON = 1e-06
NEG_FILL = -1e30


def shifted(value, axis, steps):
    count = lax.axis_size(axis)
    pairs = [(source, (source + steps) % count) for source in range(count)]
    return lax.ppermute(value, axis, pairs)


def bucket_edges():
    half_count = BUCKETS // 2
    exact_count = half_count // 2
    log_levels = half_count - exact_count
    thresholds = []
    for level_index in range(1, log_levels):
        candidate = exact_count
        while (
            candidate**log_levels * exact_count**level_index
            < MAXDIST**level_index * exact_count**log_levels
        ):
            candidate = candidate + 1
        thresholds.append(candidate)
    return (half_count, exact_count, thresholds)


def relative_bucket_index(offsets):
    half_count, exact_count, thresholds = bucket_edges()
    distance = jnp.abs(offsets)
    beyond = jnp.zeros_like(offsets)
    for threshold in thresholds:
        beyond = beyond + (distance >= threshold).astype(jnp.int32)
    upper_half = jnp.where(offsets > 0, half_count, 0).astype(jnp.int32)
    return upper_half + jnp.where(distance < exact_count, distance, exact_count + beyond)


def rms_apply(values, gain_vector):
    inverse = lax.rsqrt(jnp.mean(values * values, axis=-1, keepdims=True) + EPSILON)
    return values * inverse * gain_vector


def gated_unit(gate_value, up_value):
    return jax.nn.gelu(gate_value, approximate=True) * up_value


def feed_front(residual, norm_feed, gate_weight, up_weight):
    feed_in = rms_apply(residual, norm_feed).astype(jnp.bfloat16)
    gate_value = jnp.dot(feed_in, gate_weight, preferred_element_type=jnp.float32)
    up_value = jnp.dot(feed_in, up_weight, preferred_element_type=jnp.float32)
    return (feed_in, gate_value, up_value)


def segment_ids(item_ends, owner_index, block_rows):
    places = owner_index * block_rows + jnp.arange(block_rows, dtype=jnp.int32)
    counted = (places[None, :, None] >= item_ends[:, None, :]).astype(jnp.int32)
    return (jnp.sum(counted, axis=2), places)


def pair_bias(query_places, key_positions_flat, bucket_bias_table):
    buckets = relative_bucket_index(key_positions_flat[None, :] - query_places[:, None])
    bucket_indicator = (
        buckets[None] == jnp.arange(bucket_bias_table.shape[0], dtype=jnp.int32)[:, None, None]
    ).astype(jnp.float32)
    relative_bias = jnp.einsum(
        "ing,ij->jng", bucket_indicator, bucket_bias_table, precision=lax.Precision.HIGHEST
    )
    diagonal = query_places[:, None] == key_positions_flat[None, :]
    return (relative_bias, bucket_indicator, diagonal)


def attend_block(state, queries, keys, values, attend_allowed, relative_bias):
    running_max, row_total, weighted = state
    scores = (
        jnp.einsum("sqhe,skhe->shqk", queries, keys, preferred_element_type=jnp.float32)
        + relative_bias[None]
    )
    visible_heads = attend_allowed[:, None]
    masked = jnp.where(visible_heads, scores, NEG_FILL)
    new_max = jnp.maximum(running_max, jnp.max(masked, axis=-1))
    weights = jnp.where(visible_heads, jnp.exp(masked - new_max[..., None]), 0.0)
    rescale = jnp.exp(running_max - new_max)
    row_total = row_total * rescale + jnp.sum(weights, axis=-1)
    added = jnp.einsum(
        "shqk,skhe->sqhe", weights.astype(jnp.bfloat16), values, preferred_element_type=jnp.float32
    )
    weighted = weighted * jnp.transpose(rescale, (0, 2, 1))[..., None] + added
    return (new_max, row_total, weighted)


def back_block(
    queries, keys, values, attend_allowed, relative_bias, log_total, row_delta, grad_context
):
    scores = (
        jnp.einsum("sqhe,skhe->shqk", queries, keys, preferred_element_type=jnp.float32)
        + relative_bias[None]
    )
    visible_heads = attend_allowed[:, None]
    probs_wide = jnp.exp(jnp.where(visible_heads, scores - log_total[..., None], NEG_FILL))
    grad_probs = jnp.einsum(
        "sqhe,skhe->shqk", grad_context, values, preferred_element_type=jnp.float32
    )
    grad_scores = (probs_wide * (grad_probs - row_delta[..., None])).astype(jnp.bfloat16)
    grad_queries = jnp.einsum(
        "shqk,skhe->sqhe", grad_scores, keys, preferred_element_type=jnp.float32
    )
    grad_keys = jnp.einsum(
        "shqk,sqhe->skhe", grad_scores, queries, preferred_element_type=jnp.float32
    )
    grad_values = jnp.einsum(
        "shqk,sqhe->skhe",
        probs_wide.astype(jnp.bfloat16),
        grad_context,
        preferred_element_type=jnp.float32,
    )
    return (grad_queries, grad_keys, grad_values, jnp.sum(grad_scores.astype(jnp.float32), axis=0))


def body(
    hidden_in,
    item_lengths,
    live_mask,
    cotangent,
    query_weight,
    key_weight,
    value_weight,
    output_weight,
    bucket_bias_table,
    norm_attention,
    norm_feed,
    gate_weight,
    up_weight,
    down_weight,
):
    streams, block_rows, model_width = hidden_in.shape
    total_rows = streams * block_rows
    inner_width = query_weight.shape[1]
    cycle_size = lax.axis_size("blk")
    own_index = lax.axis_index("blk")
    item_ends = jnp.cumsum(item_lengths, axis=1)
    segment_query, query_places = segment_ids(item_ends, own_index, block_rows)
    flat_in = hidden_in.reshape(total_rows, model_width).astype(jnp.float32)
    attn_in = rms_apply(flat_in, norm_attention).astype(jnp.bfloat16)

    def project(matrix):
        product = jnp.dot(attn_in, matrix, preferred_element_type=jnp.float32)
        return product.astype(jnp.bfloat16).reshape(streams, block_rows, HEADS, HD)

    queries = project(query_weight)
    keys = project(key_weight)
    values = project(value_weight)
    live_own = live_mask.astype(jnp.bfloat16)

    def pair_setup(keys_live, owner_index):
        segment_key, key_positions_flat = segment_ids(item_ends, owner_index, block_rows)
        relative_bias, bucket_indicator, diagonal = pair_bias(
            query_places, key_positions_flat, bucket_bias_table
        )
        attend_allowed = (segment_query[:, :, None] == segment_key[:, None, :]) & (
            (keys_live[:, None, :] > 0.5) | diagonal[None]
        )
        shares = (segment_query[:, -1] >= segment_key[:, 0]) & (
            segment_key[:, -1] >= segment_query[:, 0]
        )
        return (relative_bias, bucket_indicator, attend_allowed, shares)

    def visit_forward(state, keys_now, values_now, live_now, owner_index):
        relative_bias, bucket_indicator, attend_allowed, shares = pair_setup(live_now, owner_index)
        return attend_block(state, queries, keys_now, values_now, attend_allowed, relative_bias)

    state = (
        jnp.full((streams, HEADS, block_rows), NEG_FILL, jnp.float32),
        jnp.zeros((streams, HEADS, block_rows), jnp.float32),
        jnp.zeros((streams, block_rows, HEADS, HD), jnp.float32),
    )
    state = visit_forward(state, keys, values, live_own, own_index)
    kept_blocks = ()

    def forward_turn(cycle_turn, loop_state):
        state_now, keys_now, values_now, live_now, kept_now = loop_state
        keys_now, values_now, live_now = shifted((keys_now, values_now, live_now), "blk", 1)
        state_now = visit_forward(
            state_now, keys_now, values_now, live_now, (own_index - cycle_turn) % cycle_size
        )
        return (state_now, keys_now, values_now, live_now, kept_now)

    state, unused_keys, unused_values, unused_live, kept_blocks = lax.fori_loop(
        1, cycle_size, forward_turn, (state, keys, values, live_own, kept_blocks)
    )
    running_max, row_total, weighted = state
    log_total = running_max + jnp.log(row_total)
    context_wide = weighted / jnp.transpose(row_total, (0, 2, 1))[..., None]
    context = context_wide.reshape(total_rows, inner_width).astype(jnp.bfloat16)
    residual = flat_in + jnp.dot(context, output_weight, preferred_element_type=jnp.float32)
    feed_in, gate_value, up_value = feed_front(residual, norm_feed, gate_weight, up_weight)
    hidden_act = gated_unit(gate_value, up_value).astype(jnp.bfloat16)
    output = (
        (residual + jnp.dot(hidden_act, down_weight, preferred_element_type=jnp.float32))
        .astype(jnp.bfloat16)
        .reshape(streams, block_rows, model_width)
    )
    flat_cot = cotangent.reshape(total_rows, model_width)
    feed_again, gate_again, up_again = feed_front(residual, norm_feed, gate_weight, up_weight)
    hidden_again = gated_unit(gate_again, up_again).astype(jnp.bfloat16)
    grad_down = jnp.einsum("rf,rd->fd", hidden_again, flat_cot, preferred_element_type=jnp.float32)
    grad_hidden = jnp.einsum("rd,fd->rf", flat_cot, down_weight, preferred_element_type=jnp.float32)
    unused_unit, unit_pull = jax.vjp(gated_unit, gate_again, up_again)
    grad_gate_wide, grad_up_wide = unit_pull(grad_hidden)
    grad_gate_low = grad_gate_wide.astype(jnp.bfloat16)
    grad_up_low = grad_up_wide.astype(jnp.bfloat16)
    grad_gate = jnp.einsum(
        "rd,rf->df", feed_again, grad_gate_low, preferred_element_type=jnp.float32
    )
    grad_up = jnp.einsum("rd,rf->df", feed_again, grad_up_low, preferred_element_type=jnp.float32)
    grad_feed_in = jnp.einsum(
        "rf,df->rd", grad_gate_low, gate_weight, preferred_element_type=jnp.float32
    ) + jnp.einsum("rf,df->rd", grad_up_low, up_weight, preferred_element_type=jnp.float32)
    unused_norm, norm_pull = jax.vjp(rms_apply, residual, norm_feed)
    grad_residual_norm, grad_norm_feed = norm_pull(grad_feed_in)
    grad_residual = flat_cot.astype(jnp.float32) + grad_residual_norm
    grad_branch = grad_residual.astype(jnp.bfloat16)
    grad_output_weight = jnp.einsum(
        "ri,rd->id", context, grad_branch, preferred_element_type=jnp.float32
    )
    grad_context = (
        jnp.einsum("rd,id->ri", grad_branch, output_weight, preferred_element_type=jnp.float32)
        .astype(jnp.bfloat16)
        .reshape(streams, block_rows, HEADS, HD)
    )
    row_delta = jnp.einsum("sqhe,sqhe->shq", grad_context.astype(jnp.float32), context_wide)

    def visit_backward(
        state_now, keys_now, values_now, live_now, owner_index, key_grads, value_grads
    ):
        query_grads, table_grad = state_now
        relative_bias, bucket_indicator, attend_allowed, shares = pair_setup(live_now, owner_index)
        bias_summands = back_block(
            queries,
            keys_now,
            values_now,
            attend_allowed,
            relative_bias,
            log_total,
            row_delta,
            grad_context,
        )
        query_grads = query_grads + bias_summands[0]
        key_grads = key_grads + bias_summands[1]
        value_grads = value_grads + bias_summands[2]
        table_grad = table_grad + jnp.einsum(
            "pjx,ejx->ep", bias_summands[3], bucket_indicator, precision=lax.Precision.HIGHEST
        )
        return ((query_grads, table_grad), key_grads, value_grads)

    def send_grads(key_grads, value_grads):
        return (
            shifted(key_grads.astype(jnp.bfloat16), "blk", -1).astype(key_grads.dtype),
            shifted(value_grads.astype(jnp.bfloat16), "blk", -1).astype(value_grads.dtype),
        )

    zero_grads = jnp.zeros((streams, block_rows, HEADS, HD), jnp.float32)
    back_state = (zero_grads, jnp.zeros(bucket_bias_table.shape, jnp.float32))
    back_state, key_grads, value_grads = visit_backward(
        back_state, keys, values, live_own, own_index, zero_grads, zero_grads
    )
    key_grads, value_grads = send_grads(key_grads, value_grads)

    def backward_turn(cycle_turn, loop_state):
        state_now, keys_now, values_now, live_now, key_grads, value_grads = loop_state
        keys_now, values_now, live_now = shifted((keys_now, values_now, live_now), "blk", -1)
        state_now, key_grads, value_grads = visit_backward(
            state_now,
            keys_now,
            values_now,
            live_now,
            (own_index + cycle_turn) % cycle_size,
            key_grads,
            value_grads,
        )
        key_grads, value_grads = send_grads(key_grads, value_grads)
        return (state_now, keys_now, values_now, live_now, key_grads, value_grads)

    back_state, unused_keys, unused_values, unused_live, key_grads, value_grads = lax.fori_loop(
        1, cycle_size, backward_turn, (back_state, keys, values, live_own, key_grads, value_grads)
    )
    query_grads, table_grad = back_state
    grad_queries = query_grads.astype(jnp.bfloat16).reshape(total_rows, inner_width)
    grad_keys = key_grads.astype(jnp.bfloat16).reshape(total_rows, inner_width)
    grad_values = value_grads.astype(jnp.bfloat16).reshape(total_rows, inner_width)
    grad_query = jnp.einsum("rd,ri->di", attn_in, grad_queries, preferred_element_type=jnp.float32)
    grad_key = jnp.einsum("rd,ri->di", attn_in, grad_keys, preferred_element_type=jnp.float32)
    grad_value = jnp.einsum("rd,ri->di", attn_in, grad_values, preferred_element_type=jnp.float32)
    grad_attn_in = jnp.einsum(
        "ri,di->rd", grad_queries, query_weight, preferred_element_type=jnp.float32
    )
    grad_attn_in = grad_attn_in + jnp.einsum(
        "ri,di->rd", grad_keys, key_weight, preferred_element_type=jnp.float32
    )
    grad_attn_in = grad_attn_in + jnp.einsum(
        "ri,di->rd", grad_values, value_weight, preferred_element_type=jnp.float32
    )
    unused_first, first_pull = jax.vjp(rms_apply, flat_in, norm_attention)
    grad_flat, grad_norm_attention = first_pull(grad_attn_in)
    input_gradient = (
        (grad_residual + grad_flat).astype(jnp.bfloat16).reshape(streams, block_rows, model_width)
    )
    (
        grad_query,
        grad_key,
        grad_value,
        grad_output_weight,
        table_grad,
        grad_norm_attention,
        grad_norm_feed,
        grad_gate,
        grad_up,
        grad_down,
    ) = lax.psum(
        (
            grad_query,
            grad_key,
            grad_value,
            grad_output_weight,
            table_grad,
            grad_norm_attention,
            grad_norm_feed,
            grad_gate,
            grad_up,
            grad_down,
        ),
        ("blk", "dp"),
    )
    return (
        output,
        input_gradient,
        grad_query,
        grad_key,
        grad_value,
        grad_output_weight,
        table_grad,
        grad_norm_attention,
        grad_norm_feed,
        grad_gate,
        grad_up,
        grad_down,
    )


def solution(mesh):
    return jax.shard_map(
        body,
        mesh=mesh,
        in_specs=(
            P("dp", "blk", None),
            P("dp", None),
            P("dp", "blk"),
            P("dp", "blk", None),
            P(),
            P(),
            P(),
            P(),
            P(),
            P(),
            P(),
            P(),
            P(),
            P(),
        ),
        out_specs=(
            P("dp", "blk", None),
            P("dp", "blk", None),
            P(),
            P(),
            P(),
            P(),
            P(),
            P(),
            P(),
            P(),
            P(),
            P(),
        ),
        check_vma=False,
    )
```

profile of v0, /device:TPU:0, one launch (start us, length us, event | category | flops | bytes accessed | tf_op | source)
XLA Modules:
  0.0 1094.2 jit_solution(14768908193217630293)
XLA Ops:
  40.7 299.9 %while.54 = (s32[]{:T(128)}, f32[2,6,256]{2,1,0:T(8,128)S(1)}, f32[2,6,256]{2,1,0:T(8,128)}, f32[2,256,6,64]{1,3,2,0:T(8,128)}, bf16[2,256,6,64]{1,3,2,0:T(8,128...) while((s32[]{:T(128)}, f32[2,6,256]{2,1,0:T(8,128)S(1)}, ...), condition=%wide.region_9.10_spmd.clone, body=%wide.region_5.9_spmd.clone.sunk | while | flops 367437312 | bytes 34267956 | solution.py:197
  383.9 5.7 fusion.110
  396.1 477.1 %while.55 = (s32[]{:T(128)}, f32[2,256,6,64]{1,3,2,0:T(8,128)}, f32[32,6]{0,1:T(8,128)S(1)}, bf16[2,256,6,64]{1,3,2,0:T(8,128)(2,1)}, bf16[2,256,6,64]{1,3,2,0:T...) while((s32[]{:T(128)}, f32[2,256,6,64]{1,3,2,0:T(8,128)}, ...), condition=%wide.region_16.17_spmd.clone, body=%wide.region_13.16_spmd.clone.sunk | while | flops 822313664 | bytes 52883820 | solution.py:293
  415.9 4.7 fusion.275
  424.3 4.7 collective-permute-start.3
  432.8 6.0 collective-permute-done.5
  448.0 4.7 fusion.275
  456.3 4.7 collective-permute-start.3
  464.8 6.0 collective-permute-done.5
  480.0 4.7 fusion.275
  488.4 4.7 collective-permute-start.3
  496.9 6.0 collective-permute-done.5
  512.1 4.7 fusion.275
  520.4 4.7 collective-permute-start.3
  528.9 6.0 collective-permute-done.5
  544.1 4.7 fusion.275
  552.5 4.7 collective-permute-start.3
  561.0 6.0 collective-permute-done.5
  576.2 4.7 fusion.275
  584.5 4.7 collective-permute-start.3
  593.1 6.0 collective-permute-done.5
  608.3 4.7 fusion.275
  616.6 4.7 collective-permute-start.3
  625.1 6.0 collective-permute-done.5
  640.3 4.7 fusion.275
  648.6 4.7 collective-permute-start.3
  657.2 6.0 collective-permute-done.5
  672.4 4.7 fusion.275
  680.7 4.7 collective-permute-start.3
  689.2 6.0 collective-permute-done.5
  704.4 4.7 fusion.275
  712.8 4.7 collective-permute-start.3
  721.3 6.0 collective-permute-done.5
  736.5 4.7 fusion.275
  744.8 4.7 collective-permute-start.3
  753.3 6.0 collective-permute-done.5
  768.5 4.7 fusion.275
  776.9 4.7 collective-permute-start.3
  785.4 6.0 collective-permute-done.5
  800.6 4.7 fusion.275
  808.9 4.7 collective-permute-start.3
  817.4 6.0 collective-permute-done.5
  832.6 4.7 fusion.275
  841.0 4.7 collective-permute-start.3
  849.5 6.0 collective-permute-done.5
  864.7 4.7 fusion.275
  887.0 41.0 %all-reduce = (f32[32,6]{0,1:T(8,128)}, f32[512]{0:T(512)}, f32[512]{0:T(512)}) all-reduce(f32[32,6]{0,1:T(8,128)S(1)} %get-tuple-element.729, f32[512]{0:T(512)S(1)} %get-tuple-element.918, f32[512]{0:T(512)S(1)} %copy-done.78), channel_id=1, replica_groups=mesh['blk'=16,'dp'=2] {'blk','dp'}, use_global_device_ids=true, to_apply=%region_22.23 | all-reduce | flops 1216 | bytes 9728 | tf_op jit(solution)/shard_map/psum | solution.py:328
  930.4 145.8 %all-reduce.4.cloned.1.call-done = (f32[512,384]{1,0:T(8,128)}, f32[512,384]{1,0:T(8,128)}, f32[512,384]{1,0:T(8,128)}, f32[384,512]{1,0:T(8,128)}, f32[512,1024...) async-done(((f32[512,384]{1,0:T(8,128)}, f32[512,384]{1,0:T(8,128)}, f32[512,384]{1,0:T(8,128)}, f32[384,512]{1,0:T(8,128)}, f32[512,1024]{1,0:T(8,128)}, ...) | async-done | bytes 9437200 | tf_op jit(solution)/shard_map/psum | solution.py:328
  (1255 shorter events, 662.1 us)
Async XLA Ops:
  7.2 1069.0 %all-reduce.4.cloned.1.call-start = ((), (), s32[]{:S(2)}) async-start(), calls=%async_computation | async-start | bytes 18874368 | tf_op jit(solution)/shard_map/psum | solution.py:328
  41.2 13.2 %collective-permute-start.1 = (bf16[2,256,6,64]{1,3,2,0:T(8,128)(2,1)}, bf16[2,256,6,64]{1,3,2,0:T(8,128)(2,1)}, u32[]{:S(2)}, u32[]{:S(2)}) collective-permute-start(bf16[2,256,6,64]{1,3,2,0:T(8,128)(2,1)} %get-tuple-element.1235), channel_id=1, source_target_pairs={{0,2},{2,4},{4,6},{6,8},{8,10},{10,12},{12,14},{14,16},{16,18},{18... | collective-permute-start | bytes 1179656 | tf_op jit(solution)/shard_map/while/body/eval_jaxpr/ppermute | solution.py:19
  43.8 15.0 %collective-permute-start.2 = (bf16[2,256,6,64]{1,3,2,0:T(8,128)(2,1)}, bf16[2,256,6,64]{1,3,2,0:T(8,128)(2,1)S(1)}, u32[]{:S(2)}, u32[]{:S(2)}) collective-permute-start(bf16[2,256,6,64]{1,3,2,0:T(8,128)(2,1)} %get-tuple-element.1236), channel_id=1, source_target_pairs={{0,2},{2,4},{4,6},{6,8},{8,10},{10,12},{12,14},{14,16},{16,18},{18... | collective-permute-start | bytes 1179656 | tf_op jit(solution)/shard_map/while/body/eval_jaxpr/ppermute | solution.py:19
  63.1 16.5 %collective-permute-start.2 = (bf16[2,256,6,64]{1,3,2,0:T(8,128)(2,1)}, bf16[2,256,6,64]{1,3,2,0:T(8,128)(2,1)S(1)}, u32[]{:S(2)}, u32[]{:S(2)}) collective-permute-start(bf16[2,256,6,64]{1,3,2,0:T(8,128)(2,1)} %get-tuple-element.1236), channel_id=1, source_target_pairs={{0,2},{2,4},{4,6},{6,8},{8,10},{10,12},{12,14},{14,16},{16,18},{18... | collective-permute-start | bytes 1179656 | tf_op jit(solution)/shard_map/while/body/eval_jaxpr/ppermute | solution.py:19
  84.0 15.0 %collective-permute-start.2 = (bf16[2,256,6,64]{1,3,2,0:T(8,128)(2,1)}, bf16[2,256,6,64]{1,3,2,0:T(8,128)(2,1)S(1)}, u32[]{:S(2)}, u32[]{:S(2)}) collective-permute-start(bf16[2,256,6,64]{1,3,2,0:T(8,128)(2,1)} %get-tuple-element.1236), channel_id=1, source_target_pairs={{0,2},{2,4},{4,6},{6,8},{8,10},{10,12},{12,14},{14,16},{16,18},{18... | collective-permute-start | bytes 1179656 | tf_op jit(solution)/shard_map/while/body/eval_jaxpr/ppermute | solution.py:19
  103.3 16.6 %collective-permute-start.2 = (bf16[2,256,6,64]{1,3,2,0:T(8,128)(2,1)}, bf16[2,256,6,64]{1,3,2,0:T(8,128)(2,1)S(1)}, u32[]{:S(2)}, u32[]{:S(2)}) collective-permute-start(bf16[2,256,6,64]{1,3,2,0:T(8,128)(2,1)} %get-tuple-element.1236), channel_id=1, source_target_pairs={{0,2},{2,4},{4,6},{6,8},{8,10},{10,12},{12,14},{14,16},{16,18},{18... | collective-permute-start | bytes 1179656 | tf_op jit(solution)/shard_map/while/body/eval_jaxpr/ppermute | solution.py:19
  124.2 15.0 %collective-permute-start.2 = (bf16[2,256,6,64]{1,3,2,0:T(8,128)(2,1)}, bf16[2,256,6,64]{1,3,2,0:T(8,128)(2,1)S(1)}, u32[]{:S(2)}, u32[]{:S(2)}) collective-permute-start(bf16[2,256,6,64]{1,3,2,0:T(8,128)(2,1)} %get-tuple-element.1236), channel_id=1, source_target_pairs={{0,2},{2,4},{4,6},{6,8},{8,10},{10,12},{12,14},{14,16},{16,18},{18... | collective-permute-start | bytes 1179656 | tf_op jit(solution)/shard_map/while/body/eval_jaxpr/ppermute | solution.py:19
  142.0 16.7 %collective-permute-start.2 = (bf16[2,256,6,64]{1,3,2,0:T(8,128)(2,1)}, bf16[2,256,6,64]{1,3,2,0:T(8,128)(2,1)S(1)}, u32[]{:S(2)}, u32[]{:S(2)}) collective-permute-start(bf16[2,256,6,64]{1,3,2,0:T(8,128)(2,1)} %get-tuple-element.1236), channel_id=1, source_target_pairs={{0,2},{2,4},{4,6},{6,8},{8,10},{10,12},{12,14},{14,16},{16,18},{18... | collective-permute-start | bytes 1179656 | tf_op jit(solution)/shard_map/while/body/eval_jaxpr/ppermute | solution.py:19
  163.1 15.0 %collective-permute-start.2 = (bf16[2,256,6,64]{1,3,2,0:T(8,128)(2,1)}, bf16[2,256,6,64]{1,3,2,0:T(8,128)(2,1)S(1)}, u32[]{:S(2)}, u32[]{:S(2)}) collective-permute-start(bf16[2,256,6,64]{1,3,2,0:T(8,128)(2,1)} %get-tuple-element.1236), channel_id=1, source_target_pairs={{0,2},{2,4},{4,6},{6,8},{8,10},{10,12},{12,14},{14,16},{16,18},{18... | collective-permute-start | bytes 1179656 | tf_op jit(solution)/shard_map/while/body/eval_jaxpr/ppermute | solution.py:19
  182.4 16.6 %collective-permute-start.2 = (bf16[2,256,6,64]{1,3,2,0:T(8,128)(2,1)}, bf16[2,256,6,64]{1,3,2,0:T(8,128)(2,1)S(1)}, u32[]{:S(2)}, u32[]{:S(2)}) collective-permute-start(bf16[2,256,6,64]{1,3,2,0:T(8,128)(2,1)} %get-tuple-element.1236), channel_id=1, source_target_pairs={{0,2},{2,4},{4,6},{6,8},{8,10},{10,12},{12,14},{14,16},{16,18},{18... | collective-permute-start | bytes 1179656 | tf_op jit(solution)/shard_map/while/body/eval_jaxpr/ppermute | solution.py:19
  203.3 15.0 %collective-permute-start.2 = (bf16[2,256,6,64]{1,3,2,0:T(8,128)(2,1)}, bf16[2,256,6,64]{1,3,2,0:T(8,128)(2,1)S(1)}, u32[]{:S(2)}, u32[]{:S(2)}) collective-permute-start(bf16[2,256,6,64]{1,3,2,0:T(8,128)(2,1)} %get-tuple-element.1236), channel_id=1, source_target_pairs={{0,2},{2,4},{4,6},{6,8},{8,10},{10,12},{12,14},{14,16},{16,18},{18... | collective-permute-start | bytes 1179656 | tf_op jit(solution)/shard_map/while/body/eval_jaxpr/ppermute | solution.py:19
  222.6 16.5 %collective-permute-start.2 = (bf16[2,256,6,64]{1,3,2,0:T(8,128)(2,1)}, bf16[2,256,6,64]{1,3,2,0:T(8,128)(2,1)S(1)}, u32[]{:S(2)}, u32[]{:S(2)}) collective-permute-start(bf16[2,256,6,64]{1,3,2,0:T(8,128)(2,1)} %get-tuple-element.1236), channel_id=1, source_target_pairs={{0,2},{2,4},{4,6},{6,8},{8,10},{10,12},{12,14},{14,16},{16,18},{18... | collective-permute-start | bytes 1179656 | tf_op jit(solution)/shard_map/while/body/eval_jaxpr/ppermute | solution.py:19
  241.9 15.0 %collective-permute-start.2 = (bf16[2,256,6,64]{1,3,2,0:T(8,128)(2,1)}, bf16[2,256,6,64]{1,3,2,0:T(8,128)(2,1)S(1)}, u32[]{:S(2)}, u32[]{:S(2)}) collective-permute-start(bf16[2,256,6,64]{1,3,2,0:T(8,128)(2,1)} %get-tuple-element.1236), channel_id=1, source_target_pairs={{0,2},{2,4},{4,6},{6,8},{8,10},{10,12},{12,14},{14,16},{16,18},{18... | collective-permute-start | bytes 1179656 | tf_op jit(solution)/shard_map/while/body/eval_jaxpr/ppermute | solution.py:19
  261.4 16.5 %collective-permute-start.2 = (bf16[2,256,6,64]{1,3,2,0:T(8,128)(2,1)}, bf16[2,256,6,64]{1,3,2,0:T(8,128)(2,1)S(1)}, u32[]{:S(2)}, u32[]{:S(2)}) collective-permute-start(bf16[2,256,6,64]{1,3,2,0:T(8,128)(2,1)} %get-tuple-element.1236), channel_id=1, source_target_pairs={{0,2},{2,4},{4,6},{6,8},{8,10},{10,12},{12,14},{14,16},{16,18},{18... | collective-permute-start | bytes 1179656 | tf_op jit(solution)/shard_map/while/body/eval_jaxpr/ppermute | solution.py:19
  282.3 15.0 %collective-permute-start.2 = (bf16[2,256,6,64]{1,3,2,0:T(8,128)(2,1)}, bf16[2,256,6,64]{1,3,2,0:T(8,128)(2,1)S(1)}, u32[]{:S(2)}, u32[]{:S(2)}) collective-permute-start(bf16[2,256,6,64]{1,3,2,0:T(8,128)(2,1)} %get-tuple-element.1236), channel_id=1, source_target_pairs={{0,2},{2,4},{4,6},{6,8},{8,10},{10,12},{12,14},{14,16},{16,18},{18... | collective-permute-start | bytes 1179656 | tf_op jit(solution)/shard_map/while/body/eval_jaxpr/ppermute | solution.py:19
  301.7 16.5 %collective-permute-start.2 = (bf16[2,256,6,64]{1,3,2,0:T(8,128)(2,1)}, bf16[2,256,6,64]{1,3,2,0:T(8,128)(2,1)S(1)}, u32[]{:S(2)}, u32[]{:S(2)}) collective-permute-start(bf16[2,256,6,64]{1,3,2,0:T(8,128)(2,1)} %get-tuple-element.1236), channel_id=1, source_target_pairs={{0,2},{2,4},{4,6},{6,8},{8,10},{10,12},{12,14},{14,16},{16,18},{18... | collective-permute-start | bytes 1179656 | tf_op jit(solution)/shard_map/while/body/eval_jaxpr/ppermute | solution.py:19
  322.6 15.0 %collective-permute-start.2 = (bf16[2,256,6,64]{1,3,2,0:T(8,128)(2,1)}, bf16[2,256,6,64]{1,3,2,0:T(8,128)(2,1)S(1)}, u32[]{:S(2)}, u32[]{:S(2)}) collective-permute-start(bf16[2,256,6,64]{1,3,2,0:T(8,128)(2,1)} %get-tuple-element.1236), channel_id=1, source_target_pairs={{0,2},{2,4},{4,6},{6,8},{8,10},{10,12},{12,14},{14,16},{16,18},{18... | collective-permute-start | bytes 1179656 | tf_op jit(solution)/shard_map/while/body/eval_jaxpr/ppermute | solution.py:19
  367.5 25.5 %collective-permute-start.8 = (bf16[2,256,6,64]{1,3,2,0:T(8,128)(2,1)}, bf16[2,256,6,64]{1,3,2,0:T(8,128)(2,1)}, u32[]{:S(2)}, u32[]{:S(2)}) collective-permute-start(bf16[2,256,6,64]{1,3,2,0:T(8,128)(2,1)} %fusion.106), channel_id=1, source_target_pairs={{0,30},{2,0},{4,2},{6,4},{8,6},{10,8},{12,10},{14,12},{16,14},{18,... | collective-permute-start | bytes 1179656 | tf_op jit(solution)/shard_map/ppermute | solution.py:19
  373.5 21.4 %collective-permute-start.9 = (bf16[2,256,6,64]{1,3,2,0:T(8,128)(2,1)}, bf16[2,256,6,64]{1,3,2,0:T(8,128)(2,1)}, u32[]{:S(2)}, u32[]{:S(2)}) collective-permute-start(bf16[2,256,6,64]{1,3,2,0:T(8,128)(2,1)} %fusion.107), channel_id=1, source_target_pairs={{0,30},{2,0},{4,2},{6,4},{8,6},{10,8},{12,10},{14,12},{16,14},{18,... | collective-permute-start | bytes 1179656 | tf_op jit(solution)/shard_map/ppermute | solution.py:19
  410.1 12.7 %collective-permute-start.6 = (bf16[2,256,6,64]{1,3,2,0:T(8,128)(2,1)S(1)}, bf16[2,256,6,64]{1,3,2,0:T(8,128)(2,1)S(1)}, u32[]{:S(2)}, u32[]{:S(2)}) collective-permute-start(bf16[2,256,6,64]{1,3,2,0:T(8,128)(2,1)S(1)} %fusion.276), channel_id=1, source_target_pairs={{0,30},{2,0},{4,2},{6,4},{8,6},{10,8},{12,10},{14,12},{16,14},{18,... | collective-permute-start | bytes 1179656 | tf_op jit(solution)/shard_map/while/body/eval_jaxpr/ppermute | solution.py:19
  424.3 15.3 %collective-permute-start.3 = (bf16[2,256,6,64]{1,3,2,0:T(8,128)(2,1)}, bf16[2,256,6,64]{1,3,2,0:T(8,128)(2,1)S(1)}, u32[]{:S(2)}, u32[]{:S(2)}) collective-permute-start(bf16[2,256,6,64]{1,3,2,0:T(8,128)(2,1)} %get-tuple-element.1293), channel_id=1, source_target_pairs={{0,30},{2,0},{4,2},{6,4},{8,6},{10,8},{12,10},{14,12},{16,14},{18,... | collective-permute-start | bytes 1179656 | tf_op jit(solution)/shard_map/while/body/eval_jaxpr/ppermute | solution.py:19
  442.1 12.7 %collective-permute-start.6 = (bf16[2,256,6,64]{1,3,2,0:T(8,128)(2,1)S(1)}, bf16[2,256,6,64]{1,3,2,0:T(8,128)(2,1)S(1)}, u32[]{:S(2)}, u32[]{:S(2)}) collective-permute-start(bf16[2,256,6,64]{1,3,2,0:T(8,128)(2,1)S(1)} %fusion.276), channel_id=1, source_target_pairs={{0,30},{2,0},{4,2},{6,4},{8,6},{10,8},{12,10},{14,12},{16,14},{18,... | collective-permute-start | bytes 1179656 | tf_op jit(solution)/shard_map/while/body/eval_jaxpr/ppermute | solution.py:19
  456.3 15.3 %collective-permute-start.3 = (bf16[2,256,6,64]{1,3,2,0:T(8,128)(2,1)}, bf16[2,256,6,64]{1,3,2,0:T(8,128)(2,1)S(1)}, u32[]{:S(2)}, u32[]{:S(2)}) collective-permute-start(bf16[2,256,6,64]{1,3,2,0:T(8,128)(2,1)} %get-tuple-element.1293), channel_id=1, source_target_pairs={{0,30},{2,0},{4,2},{6,4},{8,6},{10,8},{12,10},{14,12},{16,14},{18,... | collective-permute-start | bytes 1179656 | tf_op jit(solution)/shard_map/while/body/eval_jaxpr/ppermute | solution.py:19
  474.2 12.7 %collective-permute-start.6 = (bf16[2,256,6,64]{1,3,2,0:T(8,128)(2,1)S(1)}, bf16[2,256,6,64]{1,3,2,0:T(8,128)(2,1)S(1)}, u32[]{:S(2)}, u32[]{:S(2)}) collective-permute-start(bf16[2,256,6,64]{1,3,2,0:T(8,128)(2,1)S(1)} %fusion.276), channel_id=1, source_target_pairs={{0,30},{2,0},{4,2},{6,4},{8,6},{10,8},{12,10},{14,12},{16,14},{18,... | collective-permute-start | bytes 1179656 | tf_op jit(solution)/shard_map/while/body/eval_jaxpr/ppermute | solution.py:19
  488.4 15.3 %collective-permute-start.3 = (bf16[2,256,6,64]{1,3,2,0:T(8,128)(2,1)}, bf16[2,256,6,64]{1,3,2,0:T(8,128)(2,1)S(1)}, u32[]{:S(2)}, u32[]{:S(2)}) collective-permute-start(bf16[2,256,6,64]{1,3,2,0:T(8,128)(2,1)} %get-tuple-element.1293), channel_id=1, source_target_pairs={{0,30},{2,0},{4,2},{6,4},{8,6},{10,8},{12,10},{14,12},{16,14},{18,... | collective-permute-start | bytes 1179656 | tf_op jit(solution)/shard_map/while/body/eval_jaxpr/ppermute | solution.py:19
  506.2 12.7 %collective-permute-start.6 = (bf16[2,256,6,64]{1,3,2,0:T(8,128)(2,1)S(1)}, bf16[2,256,6,64]{1,3,2,0:T(8,128)(2,1)S(1)}, u32[]{:S(2)}, u32[]{:S(2)}) collective-permute-start(bf16[2,256,6,64]{1,3,2,0:T(8,128)(2,1)S(1)} %fusion.276), channel_id=1, source_target_pairs={{0,30},{2,0},{4,2},{6,4},{8,6},{10,8},{12,10},{14,12},{16,14},{18,... | collective-permute-start | bytes 1179656 | tf_op jit(solution)/shard_map/while/body/eval_jaxpr/ppermute | solution.py:19
  520.4 15.3 %collective-permute-start.3 = (bf16[2,256,6,64]{1,3,2,0:T(8,128)(2,1)}, bf16[2,256,6,64]{1,3,2,0:T(8,128)(2,1)S(1)}, u32[]{:S(2)}, u32[]{:S(2)}) collective-permute-start(bf16[2,256,6,64]{1,3,2,0:T(8,128)(2,1)} %get-tuple-element.1293), channel_id=1, source_target_pairs={{0,30},{2,0},{4,2},{6,4},{8,6},{10,8},{12,10},{14,12},{16,14},{18,... | collective-permute-start | bytes 1179656 | tf_op jit(solution)/shard_map/while/body/eval_jaxpr/ppermute | solution.py:19
  538.3 12.7 %collective-permute-start.6 = (bf16[2,256,6,64]{1,3,2,0:T(8,128)(2,1)S(1)}, bf16[2,256,6,64]{1,3,2,0:T(8,128)(2,1)S(1)}, u32[]{:S(2)}, u32[]{:S(2)}) collective-permute-start(bf16[2,256,6,64]{1,3,2,0:T(8,128)(2,1)S(1)} %fusion.276), channel_id=1, source_target_pairs={{0,30},{2,0},{4,2},{6,4},{8,6},{10,8},{12,10},{14,12},{16,14},{18,... | collective-permute-start | bytes 1179656 | tf_op jit(solution)/shard_map/while/body/eval_jaxpr/ppermute | solution.py:19
  552.5 15.3 %collective-permute-start.3 = (bf16[2,256,6,64]{1,3,2,0:T(8,128)(2,1)}, bf16[2,256,6,64]{1,3,2,0:T(8,128)(2,1)S(1)}, u32[]{:S(2)}, u32[]{:S(2)}) collective-permute-start(bf16[2,256,6,64]{1,3,2,0:T(8,128)(2,1)} %get-tuple-element.1293), channel_id=1, source_target_pairs={{0,30},{2,0},{4,2},{6,4},{8,6},{10,8},{12,10},{14,12},{16,14},{18,... | collective-permute-start | bytes 1179656 | tf_op jit(solution)/shard_map/while/body/eval_jaxpr/ppermute | solution.py:19
  570.3 12.7 %collective-permute-start.6 = (bf16[2,256,6,64]{1,3,2,0:T(8,128)(2,1)S(1)}, bf16[2,256,6,64]{1,3,2,0:T(8,128)(2,1)S(1)}, u32[]{:S(2)}, u32[]{:S(2)}) collective-permute-start(bf16[2,256,6,64]{1,3,2,0:T(8,128)(2,1)S(1)} %fusion.276), channel_id=1, source_target_pairs={{0,30},{2,0},{4,2},{6,4},{8,6},{10,8},{12,10},{14,12},{16,14},{18,... | collective-permute-start | bytes 1179656 | tf_op jit(solution)/shard_map/while/body/eval_jaxpr/ppermute | solution.py:19
  584.5 15.3 %collective-permute-start.3 = (bf16[2,256,6,64]{1,3,2,0:T(8,128)(2,1)}, bf16[2,256,6,64]{1,3,2,0:T(8,128)(2,1)S(1)}, u32[]{:S(2)}, u32[]{:S(2)}) collective-permute-start(bf16[2,256,6,64]{1,3,2,0:T(8,128)(2,1)} %get-tuple-element.1293), channel_id=1, source_target_pairs={{0,30},{2,0},{4,2},{6,4},{8,6},{10,8},{12,10},{14,12},{16,14},{18,... | collective-permute-start | bytes 1179656 | tf_op jit(solution)/shard_map/while/body/eval_jaxpr/ppermute | solution.py:19
  602.4 12.7 %collective-permute-start.6 = (bf16[2,256,6,64]{1,3,2,0:T(8,128)(2,1)S(1)}, bf16[2,256,6,64]{1,3,2,0:T(8,128)(2,1)S(1)}, u32[]{:S(2)}, u32[]{:S(2)}) collective-permute-start(bf16[2,256,6,64]{1,3,2,0:T(8,128)(2,1)S(1)} %fusion.276), channel_id=1, source_target_pairs={{0,30},{2,0},{4,2},{6,4},{8,6},{10,8},{12,10},{14,12},{16,14},{18,... | collective-permute-start | bytes 1179656 | tf_op jit(solution)/shard_map/while/body/eval_jaxpr/ppermute | solution.py:19
  616.6 15.3 %collective-permute-start.3 = (bf16[2,256,6,64]{1,3,2,0:T(8,128)(2,1)}, bf16[2,256,6,64]{1,3,2,0:T(8,128)(2,1)S(1)}, u32[]{:S(2)}, u32[]{:S(2)}) collective-permute-start(bf16[2,256,6,64]{1,3,2,0:T(8,128)(2,1)} %get-tuple-element.1293), channel_id=1, source_target_pairs={{0,30},{2,0},{4,2},{6,4},{8,6},{10,8},{12,10},{14,12},{16,14},{18,... | collective-permute-start | bytes 1179656 | tf_op jit(solution)/shard_map/while/body/eval_jaxpr/ppermute | solution.py:19
  634.5 12.7 %collective-permute-start.6 = (bf16[2,256,6,64]{1,3,2,0:T(8,128)(2,1)S(1)}, bf16[2,256,6,64]{1,3,2,0:T(8,128)(2,1)S(1)}, u32[]{:S(2)}, u32[]{:S(2)}) collective-permute-start(bf16[2,256,6,64]{1,3,2,0:T(8,128)(2,1)S(1)} %fusion.276), channel_id=1, source_target_pairs={{0,30},{2,0},{4,2},{6,4},{8,6},{10,8},{12,10},{14,12},{16,14},{18,... | collective-permute-start | bytes 1179656 | tf_op jit(solution)/shard_map/while/body/eval_jaxpr/ppermute | solution.py:19
  648.6 15.3 %collective-permute-start.3 = (bf16[2,256,6,64]{1,3,2,0:T(8,128)(2,1)}, bf16[2,256,6,64]{1,3,2,0:T(8,128)(2,1)S(1)}, u32[]{:S(2)}, u32[]{:S(2)}) collective-permute-start(bf16[2,256,6,64]{1,3,2,0:T(8,128)(2,1)} %get-tuple-element.1293), channel_id=1, source_target_pairs={{0,30},{2,0},{4,2},{6,4},{8,6},{10,8},{12,10},{14,12},{16,14},{18,... | collective-permute-start | bytes 1179656 | tf_op jit(solution)/shard_map/while/body/eval_jaxpr/ppermute | solution.py:19
  666.5 12.7 %collective-permute-start.6 = (bf16[2,256,6,64]{1,3,2,0:T(8,128)(2,1)S(1)}, bf16[2,256,6,64]{1,3,2,0:T(8,128)(2,1)S(1)}, u32[]{:S(2)}, u32[]{:S(2)}) collective-permute-start(bf16[2,256,6,64]{1,3,2,0:T(8,128)(2,1)S(1)} %fusion.276), channel_id=1, source_target_pairs={{0,30},{2,0},{4,2},{6,4},{8,6},{10,8},{12,10},{14,12},{16,14},{18,... | collective-permute-start | bytes 1179656 | tf_op jit(solution)/shard_map/while/body/eval_jaxpr/ppermute | solution.py:19
  680.7 15.3 %collective-permute-start.3 = (bf16[2,256,6,64]{1,3,2,0:T(8,128)(2,1)}, bf16[2,256,6,64]{1,3,2,0:T(8,128)(2,1)S(1)}, u32[]{:S(2)}, u32[]{:S(2)}) collective-permute-start(bf16[2,256,6,64]{1,3,2,0:T(8,128)(2,1)} %get-tuple-element.1293), channel_id=1, source_target_pairs={{0,30},{2,0},{4,2},{6,4},{8,6},{10,8},{12,10},{14,12},{16,14},{18,... | collective-permute-start | bytes 1179656 | tf_op jit(solution)/shard_map/while/body/eval_jaxpr/ppermute | solution.py:19
  698.5 12.7 %collective-permute-start.6 = (bf16[2,256,6,64]{1,3,2,0:T(8,128)(2,1)S(1)}, bf16[2,256,6,64]{1,3,2,0:T(8,128)(2,1)S(1)}, u32[]{:S(2)}, u32[]{:S(2)}) collective-permute-start(bf16[2,256,6,64]{1,3,2,0:T(8,128)(2,1)S(1)} %fusion.276), channel_id=1, source_target_pairs={{0,30},{2,0},{4,2},{6,4},{8,6},{10,8},{12,10},{14,12},{16,14},{18,... | collective-permute-start | bytes 1179656 | tf_op jit(solution)/shard_map/while/body/eval_jaxpr/ppermute | solution.py:19
  712.8 15.3 %collective-permute-start.3 = (bf16[2,256,6,64]{1,3,2,0:T(8,128)(2,1)}, bf16[2,256,6,64]{1,3,2,0:T(8,128)(2,1)S(1)}, u32[]{:S(2)}, u32[]{:S(2)}) collective-permute-start(bf16[2,256,6,64]{1,3,2,0:T(8,128)(2,1)} %get-tuple-element.1293), channel_id=1, source_target_pairs={{0,30},{2,0},{4,2},{6,4},{8,6},{10,8},{12,10},{14,12},{16,14},{18,... | collective-permute-start | bytes 1179656 | tf_op jit(solution)/shard_map/while/body/eval_jaxpr/ppermute | solution.py:19
  730.6 12.7 %collective-permute-start.6 = (bf16[2,256,6,64]{1,3,2,0:T(8,128)(2,1)S(1)}, bf16[2,256,6,64]{1,3,2,0:T(8,128)(2,1)S(1)}, u32[]{:S(2)}, u32[]{:S(2)}) collective-permute-start(bf16[2,256,6,64]{1,3,2,0:T(8,128)(2,1)S(1)} %fusion.276), channel_id=1, source_target_pairs={{0,30},{2,0},{4,2},{6,4},{8,6},{10,8},{12,10},{14,12},{16,14},{18,... | collective-permute-start | bytes 1179656 | tf_op jit(solution)/shard_map/while/body/eval_jaxpr/ppermute | solution.py:19
  744.8 15.3 %collective-permute-start.3 = (bf16[2,256,6,64]{1,3,2,0:T(8,128)(2,1)}, bf16[2,256,6,64]{1,3,2,0:T(8,128)(2,1)S(1)}, u32[]{:S(2)}, u32[]{:S(2)}) collective-permute-start(bf16[2,256,6,64]{1,3,2,0:T(8,128)(2,1)} %get-tuple-element.1293), channel_id=1, source_target_pairs={{0,30},{2,0},{4,2},{6,4},{8,6},{10,8},{12,10},{14,12},{16,14},{18,... | collective-permute-start | bytes 1179656 | tf_op jit(solution)/shard_map/while/body/eval_jaxpr/ppermute | solution.py:19
  762.7 12.7 %collective-permute-start.6 = (bf16[2,256,6,64]{1,3,2,0:T(8,128)(2,1)S(1)}, bf16[2,256,6,64]{1,3,2,0:T(8,128)(2,1)S(1)}, u32[]{:S(2)}, u32[]{:S(2)}) collective-permute-start(bf16[2,256,6,64]{1,3,2,0:T(8,128)(2,1)S(1)} %fusion.276), channel_id=1, source_target_pairs={{0,30},{2,0},{4,2},{6,4},{8,6},{10,8},{12,10},{14,12},{16,14},{18,... | collective-permute-start | bytes 1179656 | tf_op jit(solution)/shard_map/while/body/eval_jaxpr/ppermute | solution.py:19
  776.9 15.3 %collective-permute-start.3 = (bf16[2,256,6,64]{1,3,2,0:T(8,128)(2,1)}, bf16[2,256,6,64]{1,3,2,0:T(8,128)(2,1)S(1)}, u32[]{:S(2)}, u32[]{:S(2)}) collective-permute-start(bf16[2,256,6,64]{1,3,2,0:T(8,128)(2,1)} %get-tuple-element.1293), channel_id=1, source_target_pairs={{0,30},{2,0},{4,2},{6,4},{8,6},{10,8},{12,10},{14,12},{16,14},{18,... | collective-permute-start | bytes 1179656 | tf_op jit(solution)/shard_map/while/body/eval_jaxpr/ppermute | solution.py:19
  794.7 12.7 %collective-permute-start.6 = (bf16[2,256,6,64]{1,3,2,0:T(8,128)(2,1)S(1)}, bf16[2,256,6,64]{1,3,2,0:T(8,128)(2,1)S(1)}, u32[]{:S(2)}, u32[]{:S(2)}) collective-permute-start(bf16[2,256,6,64]{1,3,2,0:T(8,128)(2,1)S(1)} %fusion.276), channel_id=1, source_target_pairs={{0,30},{2,0},{4,2},{6,4},{8,6},{10,8},{12,10},{14,12},{16,14},{18,... | collective-permute-start | bytes 1179656 | tf_op jit(solution)/shard_map/while/body/eval_jaxpr/ppermute | solution.py:19
  808.9 15.3 %collective-permute-start.3 = (bf16[2,256,6,64]{1,3,2,0:T(8,128)(2,1)}, bf16[2,256,6,64]{1,3,2,0:T(8,128)(2,1)S(1)}, u32[]{:S(2)}, u32[]{:S(2)}) collective-permute-start(bf16[2,256,6,64]{1,3,2,0:T(8,128)(2,1)} %get-tuple-element.1293), channel_id=1, source_target_pairs={{0,30},{2,0},{4,2},{6,4},{8,6},{10,8},{12,10},{14,12},{16,14},{18,... | collective-permute-start | bytes 1179656 | tf_op jit(solution)/shard_map/while/body/eval_jaxpr/ppermute | solution.py:19
  826.8 12.7 %collective-permute-start.6 = (bf16[2,256,6,64]{1,3,2,0:T(8,128)(2,1)S(1)}, bf16[2,256,6,64]{1,3,2,0:T(8,128)(2,1)S(1)}, u32[]{:S(2)}, u32[]{:S(2)}) collective-permute-start(bf16[2,256,6,64]{1,3,2,0:T(8,128)(2,1)S(1)} %fusion.276), channel_id=1, source_target_pairs={{0,30},{2,0},{4,2},{6,4},{8,6},{10,8},{12,10},{14,12},{16,14},{18,... | collective-permute-start | bytes 1179656 | tf_op jit(solution)/shard_map/while/body/eval_jaxpr/ppermute | solution.py:19
  841.0 15.3 %collective-permute-start.3 = (bf16[2,256,6,64]{1,3,2,0:T(8,128)(2,1)}, bf16[2,256,6,64]{1,3,2,0:T(8,128)(2,1)S(1)}, u32[]{:S(2)}, u32[]{:S(2)}) collective-permute-start(bf16[2,256,6,64]{1,3,2,0:T(8,128)(2,1)} %get-tuple-element.1293), channel_id=1, source_target_pairs={{0,30},{2,0},{4,2},{6,4},{8,6},{10,8},{12,10},{14,12},{16,14},{18,... | collective-permute-start | bytes 1179656 | tf_op jit(solution)/shard_map/while/body/eval_jaxpr/ppermute | solution.py:19
  858.8 12.7 %collective-permute-start.6 = (bf16[2,256,6,64]{1,3,2,0:T(8,128)(2,1)S(1)}, bf16[2,256,6,64]{1,3,2,0:T(8,128)(2,1)S(1)}, u32[]{:S(2)}, u32[]{:S(2)}) collective-permute-start(bf16[2,256,6,64]{1,3,2,0:T(8,128)(2,1)S(1)} %fusion.276), channel_id=1, source_target_pairs={{0,30},{2,0},{4,2},{6,4},{8,6},{10,8},{12,10},{14,12},{16,14},{18,... | collective-permute-start | bytes 1179656 | tf_op jit(solution)/shard_map/while/body/eval_jaxpr/ppermute | solution.py:19
  (270 other events, 1830.8 us)
Sparse Core Ops, SparseCore 0:
  880.3 195.8 all-reduce.3
where the time goes:
time: 1100 us; the launch traced here: 1090 us
  matrix products  349 us (32%)
  waiting for transfers between devices  239 us (22%)
  starting transfers between devices  179 us (16%)
  local copies, waits for them, and re-layouts  168 us (15%)
  other arithmetic  98.3 us (9%)
  blocking collectives  41 us (4%)
  between operations  15.1 us (1%)
    ppermute x122, starting transfers between devices, shifted(): return lax.ppermute(value, axis, pairs)  179 us
    psum x1, waiting for transfers between devices, body(): lax.psum((grad_query, grad_key, grad_value, grad_output_weight, table_gra...  146 us
    dot_general x31, matrix products, pair_bias(): jnp.einsum('ing,ij->jng', bucket_indicator, bucket_bias_table, precision=...  114 us
    ppermute x122, waiting for transfers between devices, shifted(): return lax.ppermute(value, axis, pairs)  93 us
    while x345, local copies, waits for them, and re-layouts  92.6 us
    dot_general x16, matrix products, visit_backward(): jnp.einsum('pjx,ejx->ep', bias_summands[3], bucket_indicator, precision=l...  76.1 us
    psum x1, blocking collectives, body(): lax.psum((grad_query, grad_key, grad_value, grad_output_weight, table_gra...  41 us
    dot_general x31, local copies, waits for them, and re-layouts, pair_bias(): jnp.einsum('ing,ij->jng', bucket_indicator, bucket_bias_table, precision=...  37.1 us
  transfers between devices with their start and end apart: 123, of which 31 were waited for; matrix products, arithmetic and copies ran while one was open for 42% of the time, Pallas kernels for 0%

commit v1 on v0

v1 whole, which is shorter than its diff:
```python
import functools

import jax
import jax.numpy as jnp
from jax import lax
from jax.experimental import pallas as pl
from jax.experimental.pallas import tpu as pltpu
from jax.sharding import PartitionSpec as P

HEADS = 6
HD = 64
PAIRS = HEADS // 2
BUCKETS = 32
MAXDIST = 128
EPSILON = 1e-06
BIG = 1e30
TILE = 128
LOW = jnp.bfloat16
WIDE = jnp.float32
VMEM_LIMIT = 56 * 1024 * 1024


def bucket_edges():
    half_count = BUCKETS // 2
    exact_count = half_count // 2
    log_levels = half_count - exact_count
    thresholds = []
    for level_index in range(1, log_levels):
        candidate = exact_count
        while (
            candidate**log_levels * exact_count**level_index
            < MAXDIST**level_index * exact_count**log_levels
        ):
            candidate = candidate + 1
        thresholds.append(candidate)
    return (half_count, exact_count, thresholds)


def relative_bucket_index(offsets):
    half_count, exact_count, thresholds = bucket_edges()
    distance = jnp.abs(offsets)
    beyond = jnp.zeros_like(offsets)
    for threshold in thresholds:
        beyond = beyond + (distance >= threshold).astype(jnp.int32)
    upper_half = jnp.where(offsets > 0, half_count, 0).astype(jnp.int32)
    return upper_half + jnp.where(distance < exact_count, distance, exact_count + beyond)


FAR_BEFORE = BUCKETS // 2 - 1
FAR_AFTER = BUCKETS - 1
NEAR = 3 * TILE
TURN = 4 * TILE


def rms_apply(values, gain_vector):
    inverse = lax.rsqrt(jnp.mean(values * values, axis=-1, keepdims=True) + EPSILON)
    return values * inverse * gain_vector


def gated_unit(gate_value, up_value):
    return jax.nn.gelu(gate_value, approximate=True) * up_value


def dot_nt(left, right):
    return lax.dot_general(
        left, right, (((1,), (1,)), ((), ())), preferred_element_type=WIDE
    )


def dot_nn(left, right):
    return jnp.dot(left, right, preferred_element_type=WIDE)


def pair_columns(pair):
    return pl.ds(pl.multiple_of(pair * 2 * HD, 2 * HD), 2 * HD)


def lane_ids():
    return lax.broadcasted_iota(jnp.int32, (1, 2 * HD), 1)


def half_of(array, head_in_pair):
    keep = (lane_ids() // HD) == head_in_pair
    return jnp.where(keep, array, jnp.zeros_like(array))


def column(array, index):
    picked = jnp.where(lane_ids() == index, array, 0.0)
    return jnp.sum(picked, axis=1, keepdims=True)


def build_strip(strip_ref, near_ref, vec_ref, far_ref, before_base, after_base, chunk):
    edge = chunk - TILE
    for head in range(HEADS):
        row = jnp.broadcast_to(vec_ref[head : head + 1, :], (TILE, TURN))
        near = pltpu.roll(row, 0, 1, stride=1, stride_axis=0)[:, :NEAR]
        near_ref[head] = near
        if strip_ref is not None:
            width = strip_ref.shape[2]
            strip_ref[head, :, : edge - TILE] = jnp.full(
                (TILE, edge - TILE), far_ref[before_base + head], WIDE
            )
            strip_ref[head, :, edge - TILE : edge + 2 * TILE] = near
            rest = width - edge - 2 * TILE
            strip_ref[head, :, edge + 2 * TILE :] = jnp.full(
                (TILE, rest), far_ref[after_base + head], WIDE
            )


def tile_place(tile, core):
    per_block = 2
    return (tile // per_block) * 2 * per_block + core * per_block + tile % per_block


def strip_slice(strip_ref, head, tile, core, chunk):
    start = (chunk - TILE) - tile_place(tile, core) * TILE
    return strip_ref[head, :, pl.ds(pl.multiple_of(start, TILE), chunk)]


def project(a_ref, w_ref, qkv_ref, chunk):
    for part in range(3):
        cols = slice(part * HEADS * HD, (part + 1) * HEADS * HD)
        qkv_ref[:, cols] = dot_nn(a_ref[:chunk, :], w_ref[:, cols]).astype(LOW)


def live_row(a_ref, chunk):
    rows = a_ref[chunk : chunk + 16, :].astype(WIDE)
    return jnp.concatenate([rows[0:1, :], rows[1:2, :]], axis=1)


def forward_own_kernel(
    sc_ref, far_ref, a_ref, w_ref, vec_ref, qinfo_ref, kinfo_ref,
    qkv_ref, mask_ref, qm_ref, acc_ref, ml_ref,
    strip_ref, near_ref, gen_ref,
):
    core, first_end, quad = sc_ref[3], sc_ref[4], sc_ref[2]
    chunk = qkv_ref.shape[0]
    mine = acc_ref.shape[0]
    block = mine // 2
    inner = HEADS * HD
    project(a_ref, w_ref, qkv_ref, chunk)
    build_strip(strip_ref, near_ref, vec_ref, far_ref, 0, 8, chunk)
    live = live_row(a_ref, chunk)
    places = quad * chunk + lax.broadcasted_iota(jnp.int32, (1, chunk), 1)
    seen = (live > 0.5) & (places < first_end)
    mask_ref[0] = jnp.broadcast_to(jnp.where(seen, 0.0, -BIG), (8, chunk))
    visible = (qinfo_ref[:, 0:1] == kinfo_ref[0:1, :]) & (
        (live > 0.5) | (qinfo_ref[:, 1:2] == kinfo_ref[1:2, :])
    )
    gen_ref[...] = jnp.where(visible, 0.0, -BIG)
    for part in range(2):
        start = pl.multiple_of(core * block + part * 2 * block, block)
        q_rows = qkv_ref[pl.ds(start, block), 2 * inner :]
        for head in range(HEADS):
            pair = q_rows[:, (head // 2) * 2 * HD : (head // 2 + 1) * 2 * HD]
            qm_ref[head, part * block : (part + 1) * block, :] = half_of(pair, head % 2)
    ml_ref[...] = jnp.zeros_like(ml_ref)
    lane = lane_ids()

    def one_pair(pair, carry):
        cols = pair_columns(pair)
        k_pair = qkv_ref[:, cols]
        v_pair = qkv_ref[:, pl.ds(pl.multiple_of(inner + pair * 2 * HD, 2 * HD), 2 * HD)]
        v_ext = [jnp.where(lane // HD == hh, v_pair, jnp.ones_like(v_pair)) for hh in range(2)]
        for tile in range(mine // TILE):
            rows = slice(tile * TILE, (tile + 1) * TILE)
            ml = ml_ref[rows, :]
            sums = []
            for hh in range(2):
                head = pair * 2 + hh
                s = dot_nt(qm_ref[head, rows, :], k_pair)
                s = s + strip_slice(strip_ref, head, tile, core, chunk) + gen_ref[rows, :]
                top = jnp.max(s, axis=1, keepdims=True)
                p = jnp.exp(s - top).astype(LOW)
                pv = dot_nn(p, v_ext[hh])
                total = pv[:, HD * (1 - hh) : HD * (1 - hh) + 1]
                ml = jnp.where(lane == head, top, ml)
                ml = jnp.where(lane == head + 8, total, ml)
                sums.append(pv)
            ml_ref[rows, :] = ml
            acc_ref[rows, cols] = jnp.where(lane < HD, sums[0], sums[1])
        return carry

    lax.fori_loop(0, PAIRS, one_pair, 0)


def forward_kernel(
    sc_ref, far_ref, a_ref, w_ref, vec_ref, qinfo_ref, qm_ref, acc_in, ml_in, qkv_in, mask_in,
    qkv_ref, mask_ref, acc_ref, ml_ref,
    near_ref,
):
    valid, place, quad, core, first_end = (sc_ref[i] for i in range(5))
    chunk = qkv_ref.shape[0]
    mine = acc_ref.shape[0]
    inner = HEADS * HD
    acc_ref[...] = acc_in[...]
    ml_ref[...] = ml_in[...]
    lane = lane_ids()

    @pl.when(valid > 0)
    def _():
        project(a_ref, w_ref, qkv_ref, chunk)
        build_strip(None, near_ref, vec_ref, far_ref, 0, 8, chunk)
        live = live_row(a_ref, chunk)
        places = place * chunk + lax.broadcasted_iota(jnp.int32, (1, chunk), 1)
        seen = (live > 0.5) & (places < first_end)
        mask = jnp.where(seen, 0.0, -BIG)
        mask_ref[0] = jnp.broadcast_to(mask, (8, chunk))
        far_base = jnp.where(place > quad, 8, 0)
        fix_low = jnp.where((place == quad - 1) & (core == 0), 1.0, 0.0)
        fix_high = jnp.where((place == quad + 1) & (core == 1), 1.0, 0.0)
        rows_each = 2 * TILE

        def one_pair(pair, carry):
            cols = pair_columns(pair)
            k_pair = qkv_ref[:, cols]
            v_pair = qkv_ref[:, pl.ds(pl.multiple_of(inner + pair * 2 * HD, 2 * HD), 2 * HD)]
            v_ext = [
                jnp.where(lane // HD == hh, v_pair, jnp.ones_like(v_pair)) for hh in range(2)
            ]
            for step in range(mine // rows_each):
                rows = slice(step * rows_each, (step + 1) * rows_each)
                ml = ml_ref[rows, :]
                pen = qinfo_ref[rows, 2:3]
                sums = []
                for hh in range(2):
                    head = pair * 2 + hh
                    far = far_ref[far_base + head]
                    s = dot_nt(qm_ref[head, rows, :], k_pair) + (mask + far)
                    if step == 0:
                        fix = fix_low * (near_ref[head, :, :TILE] - far)
                        upper = jnp.concatenate(
                            [s[:TILE, : chunk - TILE], s[:TILE, chunk - TILE :] + fix], axis=1
                        )
                        s = jnp.concatenate([upper, s[TILE:]], axis=0)
                    if step == mine // rows_each - 1:
                        fix = fix_high * (near_ref[head, :, 2 * TILE :] - far)
                        lower = jnp.concatenate([s[TILE:, :TILE] + fix, s[TILE:, TILE:]], axis=1)
                        s = jnp.concatenate([s[:TILE], lower], axis=0)
                    old = column(ml, head)
                    top = jnp.maximum(old, jnp.max(s, axis=1, keepdims=True) - pen)
                    p = jnp.exp(s - (top + pen)).astype(LOW)
                    pv = dot_nn(p, v_ext[hh])
                    keep = jnp.exp(old - top)
                    total = column(ml, head + 8) * keep + pv[:, HD * (1 - hh) : HD * (1 - hh) + 1]
                    ml = jnp.where(lane == head, top, ml)
                    ml = jnp.where(lane == head + 8, total, ml)
                    sums.append((keep, pv))
                ml_ref[rows, :] = ml
                scale = jnp.where(lane < HD, sums[0][0], sums[1][0])
                added = jnp.where(lane < HD, sums[0][1], sums[1][1])
                acc_ref[rows, cols] = acc_ref[rows, cols] * scale + added
            return carry

        lax.fori_loop(0, PAIRS, one_pair, 0)


def queries_kernel(
    sc_ref, far_ref, qkv_ref, mask_ref, vec_ref, qm_ref, dom_ref, ld_ref, qinfo_ref, kinfo_ref, gen_in,
    dq_ref, diag_ref, sums_ref,
    strip_ref, near_ref, dq6_ref, grad_near_ref,
):
    quad, core = sc_ref[2], sc_ref[3]
    place = pl.program_id(0)
    chunk = qkv_ref.shape[0]
    mine = dq_ref.shape[0]
    inner = HEADS * HD
    lane = lane_ids()

    @pl.when(place == 0)
    def _():
        build_strip(strip_ref, near_ref, vec_ref, far_ref, 0, 8, chunk)
        dq6_ref[...] = jnp.zeros_like(dq6_ref)
        grad_near_ref[...] = jnp.zeros_like(grad_near_ref)

    block_of_key = lax.broadcasted_iota(jnp.int32, (chunk, 2 * HD), 0) // TILE
    gap = place - quad
    spread = jnp.where(jnp.abs(gap) <= 1, 1, 0)
    first_lane = jnp.where(spread == 1, 16 + 8 * gap, jnp.where(gap < 0, 0, 1))
    lane_of_key = first_lane + spread * block_of_key

    def operands(pair):
        cols = pair_columns(pair)
        k_pair = qkv_ref[:, cols]
        v_pair = qkv_ref[:, pl.ds(pl.multiple_of(inner + pair * 2 * HD, 2 * HD), 2 * HD)]
        k_ext = []
        for hh in range(2):
            other = lane - HD * (1 - hh)
            marks = jnp.where(other == lane_of_key, 1.0, 0.0).astype(LOW)
            k_ext.append(jnp.where(lane // HD == hh, k_pair, marks))
        return k_pair, v_pair, k_ext

    @pl.when(place == quad)
    def _():
        def one_pair(pair, carry):
            k_pair, v_pair, k_ext = operands(pair)
            for tile in range(mine // TILE):
                rows = slice(tile * TILE, (tile + 1) * TILE)
                ld = ld_ref[rows, :]
                for hh in range(2):
                    head = pair * 2 + hh
                    s = dot_nt(qm_ref[head, rows, :], k_pair)
                    s = s + strip_slice(strip_ref, head, tile, core, chunk) + gen_in[rows, :]
                    p = jnp.exp(s - column(ld, head))
                    dp = dot_nt(dom_ref[head, rows, :], v_pair)
                    ds = (p * (dp - column(ld, head + 8))).astype(LOW)
                    dq6_ref[head, rows, :] += dot_nn(ds, k_ext[hh])
                    where = tile_place(tile, core)
                    ds_wide = ds.astype(WIDE)
                    for step in range(chunk // TILE):
                        shift = step - where
                        part = ds_wide[:, step * TILE : (step + 1) * TILE]

                        @pl.when((shift >= -1) & (shift <= 1))
                        def _():
                            at = pl.ds(pl.multiple_of((shift + 1) * TILE, TILE), TILE)
                            grad_near_ref[head, :, at] += part

            return carry

        lax.fori_loop(0, PAIRS, one_pair, 0)

    @pl.when(place != quad)
    def _():
        far_base = jnp.where(place > quad, 8, 0)
        fix_low = jnp.where((place == quad - 1) & (core == 0), 1.0, 0.0)
        fix_high = jnp.where((place == quad + 1) & (core == 1), 1.0, 0.0)
        rows_each = 2 * TILE
        mask = mask_ref[0, 0:1, :]

        def one_pair(pair, carry):
            k_pair, v_pair, k_ext = operands(pair)
            for step in range(mine // rows_each):
                rows = slice(step * rows_each, (step + 1) * rows_each)
                ld = ld_ref[rows, :]
                pen = qinfo_ref[rows, 2:3]
                for hh in range(2):
                    head = pair * 2 + hh
                    far = far_ref[far_base + head]
                    s = dot_nt(qm_ref[head, rows, :], k_pair) + (mask + far)
                    if step == 0:
                        fix = fix_low * (near_ref[head, :, :TILE] - far)
                        upper = jnp.concatenate(
                            [s[:TILE, : chunk - TILE], s[:TILE, chunk - TILE :] + fix], axis=1
                        )
                        s = jnp.concatenate([upper, s[TILE:]], axis=0)
                    if step == mine // rows_each - 1:
                        fix = fix_high * (near_ref[head, :, 2 * TILE :] - far)
                        lower = jnp.concatenate([s[TILE:, :TILE] + fix, s[TILE:, TILE:]], axis=1)
                        s = jnp.concatenate([s[:TILE], lower], axis=0)
                    p = jnp.exp(s - (column(ld, head) + pen))
                    dp = dot_nt(dom_ref[head, rows, :], v_pair)
                    ds = (p * (dp - column(ld, head + 8))).astype(LOW)
                    dq6_ref[head, rows, :] += dot_nn(ds, k_ext[hh])
                    if step == 0:
                        grad_near_ref[head, :, :TILE] += fix_low * ds[
                            :TILE, chunk - TILE :
                        ].astype(WIDE)
                    if step == mine // rows_each - 1:
                        grad_near_ref[head, :, 2 * TILE :] += fix_high * ds[TILE:, :TILE].astype(
                            WIDE
                        )
            return carry

        lax.fori_loop(0, PAIRS, one_pair, 0)

    @pl.when(place == pl.num_programs(0) - 1)
    def _():
        flip = (
            lax.broadcasted_iota(jnp.int32, (TILE, TILE), 0)
            + lax.broadcasted_iota(jnp.int32, (TILE, TILE), 1)
            == TILE - 1
        ).astype(WIDE)
        diag_ref[...] = jnp.zeros_like(diag_ref)
        sums_ref[...] = jnp.zeros_like(sums_ref)
        for head in range(HEADS):
            turned = jnp.dot(
                flip, grad_near_ref[head], precision=lax.Precision.HIGHEST,
                preferred_element_type=WIDE,
            )
            wide = jnp.concatenate([turned, jnp.zeros((TILE, TURN - NEAR), WIDE)], axis=1)
            skewed = pltpu.roll(wide, 0, 1, stride=1, stride_axis=0)
            diag_ref[head : head + 1, :] = jnp.sum(skewed, axis=0, keepdims=True)
            for tile in range(mine // TILE):
                rows = slice(tile * TILE, (tile + 1) * TILE)
                sums_ref[head, tile : tile + 1, :] = jnp.sum(
                    dq6_ref[head, rows, :], axis=0, keepdims=True
                )
        for pair in range(PAIRS):
            dq_ref[:, pair * 2 * HD : (pair + 1) * 2 * HD] = jnp.where(
                lane < HD, dq6_ref[2 * pair], dq6_ref[2 * pair + 1]
            ).astype(LOW)


def keys_kernel(
    own, sc_ref, far_ref, pieces_ref, dox_ref, q_ref, kv0_ref, kv1_ref, vec_ref, kinfo_ref, rowinfo_ref, dkv_in,
    dkv_ref,
    strip_ref, near_ref, gen_ref,
):
    valid, place, quad, core = (sc_ref[i] for i in range(4))
    chunk = q_ref.shape[0]
    mine = dkv_ref.shape[0]
    block = mine // 2
    inner = HEADS * HD
    lane = lane_ids()
    if own:
        build_strip(strip_ref, near_ref, vec_ref, far_ref, 8, 0, chunk)
        visible = (kinfo_ref[:, 0:1] == rowinfo_ref[0:1, :]) & (
            (kinfo_ref[:, 3:4] > 0.5) | (kinfo_ref[:, 1:2] == rowinfo_ref[1:2, :])
        )
        gen_ref[...] = jnp.where(visible, 0.0, -BIG)
    else:
        dkv_ref[...] = dkv_in[...]

    @pl.when(valid > 0)
    def _():
        if not own:
            build_strip(None, near_ref, vec_ref, far_ref, 8, 0, chunk)
        far_base = jnp.where(place > quad, 0, 8)
        fix_low = jnp.where((place == quad - 1) & (core == 0), 1.0, 0.0)
        fix_high = jnp.where((place == quad + 1) & (core == 1), 1.0, 0.0)
        ext = dox_ref[:, inner:]
        rows_each = TILE if own else 2 * TILE

        def one_pair(pair, carry):
            cols = pair_columns(pair)
            vcols = pl.ds(pl.multiple_of(inner + pair * 2 * HD, 2 * HD), 2 * HD)
            q_pair = q_ref[:, cols]
            do_pair = dox_ref[:, cols]
            q_ext = jnp.concatenate([q_pair, ext], axis=1)
            do_ext = jnp.concatenate([do_pair, ext], axis=1)
            for step in range(mine // rows_each):
                start = step * rows_each
                rows = slice(start, start + rows_each)
                half_ref = kv0_ref if start < block else kv1_ref
                inside = slice(start % block, start % block + rows_each)
                k_rows = half_ref[inside, cols]
                v_rows = half_ref[inside, vcols]
                grads = []
                for hh in range(2):
                    head = pair * 2 + hh
                    marks = jnp.where(
                        (lane == head) | (lane == head + 6) | (lane == head + 12), 1.0, 0.0
                    )
                    if own:
                        marks = jnp.broadcast_to(marks, (rows_each, 2 * HD))
                    else:
                        for number, at in enumerate((36, 38, 39)):
                            marks = jnp.where(
                                lane == at, pieces_ref[number * 16 + far_base + head], marks
                            )
                        marks = jnp.where(lane == 37, 1.0, marks)
                        marks = jnp.where(lane == 40, kinfo_ref[rows, 2:3], marks)
                    s = dot_nt(
                        jnp.concatenate([half_of(k_rows, hh), marks.astype(LOW)], axis=1), q_ext
                    )
                    if own:
                        s = s + strip_slice(strip_ref, head, step, core, chunk) + gen_ref[rows, :]
                    else:
                        far = far_ref[far_base + head]
                        if step == 0:
                            fix = fix_low * (near_ref[head, :, :TILE] - far)
                            upper = jnp.concatenate(
                                [s[:TILE, : chunk - TILE], s[:TILE, chunk - TILE :] + fix], axis=1
                            )
                            s = jnp.concatenate([upper, s[TILE:]], axis=0)
                        if step == mine // rows_each - 1:
                            fix = fix_high * (near_ref[head, :, 2 * TILE :] - far)
                            lower = jnp.concatenate(
                                [s[TILE:, :TILE] + fix, s[TILE:, TILE:]], axis=1
                            )
                            s = jnp.concatenate([s[:TILE], lower], axis=0)
                    p = jnp.exp(s)
                    grad_v = dot_nn(p.astype(LOW), do_pair)
                    delta_marks = jnp.where(
                        (lane == head + 18) | (lane == head + 24) | (lane == head + 30), 1.0, 0.0
                    )
                    delta_marks = jnp.broadcast_to(delta_marks, (rows_each, 2 * HD)).astype(LOW)
                    dp = dot_nt(
                        jnp.concatenate([half_of(v_rows, hh), delta_marks], axis=1), do_ext
                    )
                    ds = (p * dp).astype(LOW)
                    grads.append((dot_nn(ds, q_pair), grad_v))
                grad_k = jnp.where(lane < HD, grads[0][0], grads[1][0])
                grad_v = jnp.where(lane < HD, grads[0][1], grads[1][1])
                if own:
                    dkv_ref[rows, cols] = grad_k
                    dkv_ref[rows, vcols] = grad_v
                else:
                    dkv_ref[rows, cols] += grad_k
                    dkv_ref[rows, vcols] += grad_v
            return carry

        lax.fori_loop(0, PAIRS, one_pair, 0)


def group_sum(value, plan):
    for axis, size, index, pairs in plan:
        part = value.shape[0] // size
        total = lax.dynamic_slice_in_dim(value, index * part, part, 0).astype(WIDE)
        for shift in range(1, size):
            target = (index + shift) % size
            sent = lax.dynamic_slice_in_dim(value, target * part, part, 0)
            total = total + lax.ppermute(sent, axis, pairs(shift)).astype(WIDE)
        value = total.astype(LOW)
    for axis, size, index, pairs in reversed(plan):
        gathered = [value]
        for shift in range(1, size):
            gathered.append(lax.ppermute(value, axis, pairs(shift)))
        if size == 2:
            low = jnp.where(index == 0, gathered[0], gathered[1])
            high = jnp.where(index == 0, gathered[1], gathered[0])
            value = jnp.concatenate([low, high], axis=0)
        else:
            whole = jnp.zeros((size,) + value.shape, value.dtype)
            for shift, part in enumerate(gathered):
                whole = lax.dynamic_update_slice_in_dim(
                    whole, part[None], (index - shift) % size, 0
                )
            value = whole.reshape((-1,) + value.shape[1:])
    return value.astype(WIDE)


def padded_rows(arrays, multiple):
    stacked = jnp.concatenate([a.astype(LOW) for a in arrays], axis=0)
    short = -stacked.shape[0] % multiple
    return jnp.pad(stacked, ((0, short), (0, 0)))


def body(
    hidden_in,
    item_lengths,
    live_mask,
    cotangent,
    query_weight,
    key_weight,
    value_weight,
    output_weight,
    bucket_bias_table,
    norm_attention,
    norm_feed,
    gate_weight,
    up_weight,
    down_weight,
):
    streams, block, width = hidden_in.shape
    inner = query_weight.shape[1]
    blocks = lax.axis_size("blk")
    parts = lax.axis_size("dp")
    quads = blocks // 4
    here = lax.axis_index("blk")
    core, side, quad = here % 2, (here // 2) % 2, here // 4
    mine, chunk = 2 * block, 4 * block

    across = [(k, k ^ 2) for k in range(blocks)]
    between = [(k, k ^ 1) for k in range(blocks)]
    onward = []
    for k in range(blocks):
        if k % 2 == 0:
            onward.append((k, k + 4 if k + 4 < blocks else k + 1))
        else:
            onward.append((k, k - 4 if k >= 4 else k - 1))

    def to_streams(both):
        kept = lax.dynamic_index_in_dim(both, side, 0, False)
        sent = lax.dynamic_index_in_dim(both, 1 - side, 0, False)
        got = lax.ppermute(sent, "blk", across)
        return jnp.where(side == 0, kept, got), jnp.where(side == 0, got, kept)

    def from_streams(rows):
        split = rows.reshape(2, block, rows.shape[1])
        kept = lax.dynamic_index_in_dim(split, side, 0, False)
        sent = lax.dynamic_index_in_dim(split, 1 - side, 0, False)
        got = lax.ppermute(sent, "blk", across)
        return jnp.stack([jnp.where(side == 0, kept, got), jnp.where(side == 0, got, kept)])

    def with_other_core(rows):
        got = lax.ppermute(rows, "blk", between)
        return jnp.where(core == 0, rows, got), jnp.where(core == 0, got, rows)

    live_rows = jnp.pad(live_mask.astype(LOW)[:, None, :], ((0, 0), (0, 15), (0, width - block)))
    first, second = to_streams(jnp.concatenate([hidden_in, live_rows], axis=1))
    x_low = jnp.concatenate([first[:block], second[:block]], axis=0)
    live_own = jnp.concatenate([first[block, :block], second[block, :block]])
    x = x_low.astype(WIDE)
    attn_in = rms_apply(x, norm_attention).astype(LOW)
    packed = jnp.concatenate([attn_in, jnp.pad(live_own[None, :], ((0, 15), (0, 0)))], axis=0)
    even, odd = with_other_core(packed)
    live_even, live_odd = even[mine], odd[mine]
    live_chunk = jnp.concatenate(
        [live_even[:block], live_odd[:block], live_even[block:], live_odd[block:]]
    )
    own_chunk = jnp.concatenate(
        [
            even[:block],
            odd[:block],
            even[block:mine],
            odd[block:mine],
            jnp.pad(live_chunk.reshape(2, 2 * block), ((0, 14), (0, 0))),
        ],
        axis=0,
    )

    item_ends = jnp.cumsum(item_lengths, axis=1)
    ends = lax.dynamic_index_in_dim(item_ends, side, 0, False)
    places = quad * chunk + jnp.arange(chunk, dtype=jnp.int32)
    segments = jnp.sum((places[:, None] >= ends[None, :]).astype(jnp.int32), axis=1)

    def own_part(vector):
        quarter = vector.reshape(2, 2, block)
        return lax.dynamic_index_in_dim(quarter, core, 1, False).reshape(mine)

    own_segments, own_places = own_part(segments), own_part(places)
    pen = jnp.where(own_segments > 0, BIG, 0.0)
    key_off = jnp.where((live_own > 0.5) & (own_segments == 0), 0.0, -BIG)
    qinfo = jnp.stack(
        [own_segments.astype(WIDE), own_places.astype(WIDE), pen, live_own.astype(WIDE)], axis=1
    )
    qinfo = jnp.pad(qinfo, ((0, 0), (0, 4)))
    kinfo = jnp.stack(
        [own_segments.astype(WIDE), own_places.astype(WIDE), key_off, live_own.astype(WIDE)], axis=1
    )
    kinfo = jnp.pad(kinfo, ((0, 0), (0, 4)))
    rowinfo = jnp.stack(
        [segments.astype(WIDE), places.astype(WIDE), live_chunk.astype(WIDE)], axis=0
    )
    rowinfo = jnp.pad(rowinfo, ((0, 5), (0, 0)))

    turns = jnp.arange(TURN, dtype=jnp.int32)
    offsets = jnp.where(turns < NEAR, turns, turns - TURN) - TILE

    def bias_of(offset):
        chosen = relative_bucket_index(offset)[:, None] == jnp.arange(BUCKETS, dtype=jnp.int32)
        return jnp.einsum(
            "bh,ob->ho", bucket_bias_table, chosen.astype(WIDE), precision=lax.Precision.HIGHEST
        )

    vec = jnp.pad(bias_of(offsets), ((0, 2), (0, 0)))
    vec_back = jnp.pad(bias_of(-offsets), ((0, 2), (0, 0)))
    far = jnp.zeros((16,), WIDE)
    far = far.at[:HEADS].set(bucket_bias_table[FAR_BEFORE])
    far = far.at[8 : 8 + HEADS].set(bucket_bias_table[FAR_AFTER])

    def in_pieces(values):
        high = lax.reduce_precision(values, 8, 7)
        mid = lax.reduce_precision(values - high, 8, 7)
        low = lax.reduce_precision(values - high - mid, 8, 7)
        return high, mid, low

    pieces = jnp.concatenate(in_pieces(far))
    w_all = jnp.concatenate([key_weight, value_weight, query_weight], axis=1)

    def scalars(valid, place):
        zero = jnp.zeros((), jnp.int32)
        out = jnp.where(valid, place, quads)
        return jnp.stack(
            [valid.astype(jnp.int32), place, quad, core, ends[0], out, zero, zero]
        ).astype(jnp.int32)

    own_scalars = scalars(jnp.bool_(True), quad)
    smem = pl.BlockSpec(memory_space=pltpu.SMEM)
    vmem = pl.BlockSpec(memory_space=pltpu.VMEM)
    anywhere = pl.BlockSpec(memory_space=pl.ANY)
    params = pltpu.CompilerParams(vmem_limit_bytes=VMEM_LIMIT)
    shape = jax.ShapeDtypeStruct
    qkv_shape = shape(((quads + 1) * chunk, 3 * inner), LOW)
    mask_shape = shape((quads + 1, 8, chunk), WIDE)
    strip_shape = pltpu.VMEM((HEADS, TILE, 2 * chunk - TILE), WIDE)
    near_shape = pltpu.VMEM((HEADS, TILE, NEAR), WIDE)
    gen_shape = pltpu.VMEM((mine, chunk), WIDE)
    pair_shape = shape((HEADS, mine, 2 * HD), LOW)

    def at_out(columns):
        return pl.BlockSpec((chunk, columns), lambda i, sc: (sc[5], 0))

    mask_out = pl.BlockSpec((1, 8, chunk), lambda i, sc: (sc[5], 0, 0))

    def cost(products, exps):
        pairs = mine * chunk * HEADS
        return pl.CostEstimate(
            flops=2 * 4 * HD * products * pairs, bytes_accessed=8 << 20, transcendentals=exps * pairs
        )

    qkv, masks, qm, acc, ml = pl.pallas_call(
        forward_own_kernel,
        grid_spec=pltpu.PrefetchScalarGridSpec(
            num_scalar_prefetch=1,
            grid=(1,),
            in_specs=[smem] + [vmem] * 5,
            out_specs=(at_out(3 * inner), mask_out, vmem, vmem, vmem),
            scratch_shapes=[strip_shape, near_shape, gen_shape],
        ),
        out_shape=(
            qkv_shape, mask_shape, pair_shape, shape((mine, inner), WIDE), shape((mine, 2 * HD), WIDE),
        ),
        compiler_params=params,
        cost_estimate=cost(2, 1),
        name="attend_own",
    )(own_scalars, far, own_chunk, w_all, vec, qinfo, rowinfo)

    def forward_step(state, a_chunk, valid, place):
        qkv, masks, acc, ml = state
        return pl.pallas_call(
            forward_kernel,
            grid_spec=pltpu.PrefetchScalarGridSpec(
                num_scalar_prefetch=1,
                grid=(1,),
                in_specs=[smem] + [vmem] * 7 + [anywhere, anywhere],
                out_specs=(at_out(3 * inner), mask_out, vmem, vmem),
                scratch_shapes=[near_shape],
            ),
            out_shape=(
                qkv_shape, mask_shape, shape((mine, inner), WIDE), shape((mine, 2 * HD), WIDE),
            ),
            input_output_aliases={9: 0, 10: 1, 7: 2, 8: 3},
            compiler_params=params,
            cost_estimate=cost(2, 1),
            name="attend_other",
        )(scalars(valid, place), far, a_chunk, w_all, vec, qinfo, qm, acc, ml, qkv, masks)

    def arrivals(chunk_array):
        held = chunk_array
        for step in range(1, quads):
            held = lax.ppermute(held, "blk", onward)
            other = lax.ppermute(held, "blk", between)
            below, above = quad - step, quad + step
            direct = jnp.where(core == 0, below, above)
            swapped = jnp.where(core == 0, above, below)
            for array, place in ((held, direct), (other, swapped)):
                yield array, (place >= 0) & (place < quads), place

    state = (qkv, masks, acc, ml)
    for a_chunk, valid, place in arrivals(own_chunk):
        state = forward_step(state, a_chunk, valid, place)
    qkv, masks, acc, ml = state

    row_total = ml[:, 8 : 8 + HEADS]
    log_total = ml[:, :HEADS] + jnp.log(row_total)
    context_wide = acc / jnp.repeat(row_total, HD, axis=1)
    context = context_wide.astype(LOW)

    cot_first, cot_second = to_streams(cotangent)
    flat_cot = jnp.concatenate([cot_first, cot_second], axis=0)
    residual = x + dot_nn(context, output_weight)
    feed_in = rms_apply(residual, norm_feed).astype(LOW)
    gate_value = dot_nn(feed_in, gate_weight)
    up_value = dot_nn(feed_in, up_weight)
    hidden_act = gated_unit(gate_value, up_value).astype(LOW)
    output = (residual + dot_nn(hidden_act, down_weight)).astype(LOW)
    grad_hidden = dot_nt(flat_cot, down_weight)
    unused_unit, unit_pull = jax.vjp(gated_unit, gate_value, up_value)
    grad_gate_wide, grad_up_wide = unit_pull(grad_hidden)
    grad_gate_low, grad_up_low = grad_gate_wide.astype(LOW), grad_up_wide.astype(LOW)
    grad_feed_in = dot_nt(grad_gate_low, gate_weight) + dot_nt(grad_up_low, up_weight)
    unused_norm, norm_pull = jax.vjp(rms_apply, residual, norm_feed)
    grad_residual_norm, grad_norm_feed = norm_pull(grad_feed_in)
    grad_residual = flat_cot.astype(WIDE) + grad_residual_norm
    grad_branch = grad_residual.astype(LOW)
    grad_context = dot_nt(grad_branch, output_weight).astype(LOW)
    row_delta = jnp.sum(
        (grad_context.astype(WIDE) * context_wide).reshape(mine, HEADS, HD), axis=2
    )

    ones = jnp.ones((mine, 1), WIDE)
    ext = jnp.concatenate(
        [*in_pieces(-log_total), *in_pieces(-row_delta), ones, -pen[:, None], ones, ones, ones],
        axis=1,
    )
    ext = jnp.pad(ext, ((0, 0), (0, 2 * HD - ext.shape[1]))).astype(LOW)
    do_ext = jnp.concatenate([grad_context, ext], axis=1)
    do_even, do_odd = with_other_core(do_ext)
    do_chunk = jnp.concatenate(
        [do_even[:block], do_odd[:block], do_even[block:], do_odd[block:]], axis=0
    )

    def tn(left, right):
        return lax.dot_general(left, right, (((0,), (0,)), ((), ())), preferred_element_type=WIDE)

    def group(axis, size, index, pair_of):
        return (axis, size, index, pair_of)

    plan = [
        group("blk", 2, core, lambda s: between),
        group("blk", 2, side, lambda s: across),
        group("dp", parts, lax.axis_index("dp"), lambda s: [(k, (k + s) % parts) for k in range(parts)]),
        group(
            "blk", quads, quad,
            lambda s: [(k, (k + 4 * s) % blocks) for k in range(blocks)],
        ),
    ]

    grad_gate = tn(feed_in, grad_gate_low)
    grad_up = tn(feed_in, grad_up_low)
    grad_down = tn(hidden_act, flat_cot)
    grad_output_weight = tn(context, grad_branch)
    feed_rows = padded_rows(
        [
            grad_gate[:, :width], grad_gate[:, width:], grad_up[:, :width], grad_up[:, width:],
            grad_down, grad_output_weight, grad_norm_feed[None, :],
        ],
        512,
    )
    feed_sum = group_sum(feed_rows, plan)

    ld = jnp.zeros((mine, 2 * HD), WIDE)
    ld = ld.at[:, :HEADS].set(log_total).at[:, 8 : 8 + HEADS].set(row_delta)
    lane_half = (jnp.arange(2 * HD) // HD)[None, :]
    dom = jnp.stack(
        [
            jnp.where(
                lane_half == head % 2,
                grad_context[:, (head // 2) * 2 * HD : (head // 2 + 1) * 2 * HD],
                jnp.zeros((), LOW),
            )
            for head in range(HEADS)
        ]
    )
    visible = (own_segments[:, None] == segments[None, :]) & (
        (live_chunk[None, :] > 0.5) | (own_places[:, None] == places[None, :])
    )
    gen = jnp.where(visible, 0.0, -BIG)
    grad_queries, diag, sums = pl.pallas_call(
        queries_kernel,
        grid_spec=pltpu.PrefetchScalarGridSpec(
            num_scalar_prefetch=1,
            grid=(quads,),
            in_specs=[
                smem,
                pl.BlockSpec((chunk, 2 * inner), lambda i, sc: (i, 0)),
                pl.BlockSpec((1, 8, chunk), lambda i, sc: (i, 0, 0)),
            ]
            + [vmem] * 7,
            out_specs=(vmem, vmem, vmem),
            scratch_shapes=[
                strip_shape, near_shape, pltpu.VMEM((HEADS, mine, 2 * HD), WIDE),
                pltpu.VMEM((HEADS, TILE, NEAR), WIDE),
            ],
        ),
        out_shape=(shape((mine, inner), LOW), shape((8, TURN), WIDE), shape((HEADS, 8, 2 * HD), WIDE)),
        compiler_params=params,
        cost_estimate=cost(3 * 4, 4),
        name="grad_queries",
    )(own_scalars, far, qkv, masks, vec, qm, dom, ld, qinfo, rowinfo, gen)

    steps = jnp.arange(TURN, dtype=jnp.int32) - (TILE - 1) - TILE
    chosen = relative_bucket_index(steps)[:, None] == jnp.arange(BUCKETS, dtype=jnp.int32)[None, :]
    table_grad = jnp.einsum(
        "ho,ob->bh", diag[:HEADS], chosen.astype(WIDE), precision=lax.Precision.HIGHEST
    )
    tiles = jnp.arange(mine // TILE, dtype=jnp.int32)
    where = (tiles // 2) * 4 + core * 2 + tiles % 2
    lanes = jnp.arange(HD, dtype=jnp.int32)
    relative = (lanes - 16)[None, :] - where[:, None]
    inside = (lanes >= 8) & (lanes < 32)
    before = (lanes == 0)[None, :] | (inside[None, :] & (relative < -1))
    after = (lanes == 1)[None, :] | (inside[None, :] & (relative > 1))
    block_sums = jnp.stack(
        [sums[head, : mine // TILE, HD * (1 - head % 2) : HD * (2 - head % 2)] for head in range(HEADS)]
    )
    table_grad = table_grad.at[FAR_BEFORE].add(
        jnp.sum(jnp.where(before[None], block_sums, 0.0), axis=(1, 2))
    )
    table_grad = table_grad.at[FAR_AFTER].add(
        jnp.sum(jnp.where(after[None], block_sums, 0.0), axis=(1, 2))
    )

    def keys_step(own, dkv, do_array, valid, place):
        sc = scalars(valid, place)
        sc = sc.at[6].set(jnp.clip(place, 0, quads - 1))
        return pl.pallas_call(
            functools.partial(keys_kernel, own),
            grid_spec=pltpu.PrefetchScalarGridSpec(
                num_scalar_prefetch=1,
                grid=(1,),
                in_specs=[
                    smem,
                    smem,
                    vmem,
                    pl.BlockSpec((chunk, inner), lambda i, sc: (sc[6], 2)),
                    pl.BlockSpec((block, 2 * inner), lambda i, sc: (4 * sc[2] + sc[3], 0)),
                    pl.BlockSpec((block, 2 * inner), lambda i, sc: (4 * sc[2] + sc[3] + 2, 0)),
                    vmem,
                    vmem,
                    vmem,
                    vmem,
                ],
                out_specs=vmem,
                scratch_shapes=[strip_shape, near_shape, gen_shape],
            ),
            out_shape=shape((mine, 2 * inner), WIDE),
            input_output_aliases={10: 0},
            compiler_params=params,
            cost_estimate=cost(4, 1),
            name="grad_keys_own" if own else "grad_keys_other",
        )(sc, far, pieces, do_array, qkv, qkv, qkv, vec_back, kinfo, rowinfo, dkv)

    dkv = jnp.zeros((mine, 2 * inner), WIDE)
    dkv = keys_step(True, dkv, do_chunk, jnp.bool_(True), quad)
    for do_array, valid, place in arrivals(do_chunk):
        dkv = keys_step(False, dkv, do_array, valid, place)
    grad_keys = dkv[:, :inner].astype(LOW)
    grad_values = dkv[:, inner:].astype(LOW)

    grad_attn_in = dot_nt(grad_queries, query_weight)
    grad_attn_in = grad_attn_in + dot_nt(grad_keys, key_weight)
    grad_attn_in = grad_attn_in + dot_nt(grad_values, value_weight)
    unused_first, first_pull = jax.vjp(rms_apply, x, norm_attention)
    grad_flat, grad_norm_attention = first_pull(grad_attn_in)
    input_gradient = (grad_residual + grad_flat).astype(LOW)

    small = jnp.concatenate(
        [
            grad_norm_attention,
            jnp.zeros((2 * inner - width,), WIDE),
            table_grad.reshape(-1),
            jnp.zeros((inner - table_grad.size,), WIDE),
        ]
    ).reshape(3, inner)
    attention_rows = padded_rows(
        [
            tn(attn_in, grad_queries), tn(attn_in, grad_keys), tn(attn_in, grad_values), small,
        ],
        256,
    )
    attention_sum = group_sum(attention_rows, plan)

    hidden = gate_weight.shape[1]
    base = 4 * width
    return (
        from_streams(output),
        from_streams(input_gradient),
        attention_sum[:width],
        attention_sum[width : 2 * width],
        attention_sum[2 * width : 3 * width],
        feed_sum[base + hidden : base + hidden + inner],
        attention_sum[3 * width + 2].reshape(-1)[: BUCKETS * HEADS].reshape(BUCKETS, HEADS),
        attention_sum[3 * width : 3 * width + 2].reshape(-1)[:width],
        feed_sum[base + hidden + inner],
        jnp.concatenate([feed_sum[:width], feed_sum[width : 2 * width]], axis=1),
        jnp.concatenate([feed_sum[2 * width : 3 * width], feed_sum[3 * width : base]], axis=1),
        feed_sum[base : base + hidden],
    )


def solution(mesh):
    return jax.shard_map(
        body,
        mesh=mesh,
        in_specs=(
            P("dp", "blk", None),
            P("dp", None),
            P("dp", "blk"),
            P("dp", "blk", None),
            P(),
            P(),
            P(),
            P(),
            P(),
            P(),
            P(),
            P(),
            P(),
            P(),
        ),
        out_specs=(
            P("dp", "blk", None),
            P("dp", "blk", None),
            P(),
            P(),
            P(),
            P(),
            P(),
            P(),
            P(),
            P(),
            P(),
            P(),
        ),
        check_vma=False,
    )
```

time: 1100 us -> 463 us (0.42)
  matrix products: 349 us -> 23.8 us
  Pallas kernels: 0 us -> 184 us
  waiting for transfers between devices: 239 us -> 63.9 us
  starting transfers between devices: 179 us -> 65.8 us
  local copies, waits for them, and re-layouts: 168 us -> 62.3 us
  other arithmetic: 98.3 us -> 52.7 us
  blocking collectives: 41 us -> 0 us
  between operations: 15.1 us -> 2.63 us
    dot_general x179 -> x21, matrix products: 349 us -> 23.8 us  [the longest x7 9.46 us: dot_nt(): lax.dot_general(left, right, (((1,), (1,)), ((), ())), preferred_element_...]
    pallas_call x0 -> x15, Pallas kernels: none -> 184 us  [the longest x7 69.9 us: keys_step(): pl.pallas_call(functools.partial(keys_kernel, own), grid_spec=pltpu.Prefe...]
    psum x1 -> x0, waiting for transfers between devices: 146 us -> none  [body(): lax.psum((grad_query, grad_key, grad_value, grad_output_weight, table_gra...]
    ppermute x122 -> x42, starting transfers between devices: 179 us -> 65.8 us  [the longest x6 18.3 us: arrivals(): other = lax.ppermute(held, 'blk', between)]
    while x345 -> x0, local copies, waits for them, and re-layouts: 92.6 us -> none
    psum x1 -> x0, blocking collectives: 41 us -> none  [body(): lax.psum((grad_query, grad_key, grad_value, grad_output_weight, table_gra...]
    dot_general x31 -> x0, local copies, waits for them, and re-layouts: 37.1 us -> none  [pair_bias(): jnp.einsum('ing,ij->jng', bucket_indicator, bucket_bias_table, precision=...]
    ppermute x122 -> x42, waiting for transfers between devices: 93 us -> 63.9 us  [the longest x12 32.2 us: group_sum(): gathered.append(lax.ppermute(value, axis, pairs(shift)))]
  transfers between devices with their start and end apart: 123 -> 42, of which waited for: 31 -> 14; matrix products, arithmetic and copies ran while one was open for 42% -> 20% of each run, Pallas kernels for 0% -> 37%
where the time goes in v1:
time: 463 us; the launch traced here: 455 us
  Pallas kernels  184 us (40%)
  starting transfers between devices  65.8 us (14%)
  waiting for transfers between devices  63.9 us (14%)
  local copies, waits for them, and re-layouts  62.3 us (13%)
  other arithmetic  52.7 us (11%)
  matrix products  23.8 us (5%)
    pallas_call x7, Pallas kernels, keys_step(): pl.pallas_call(functools.partial(keys_kernel, own), grid_spec=pltpu.Prefe...  69.9 us
    pallas_call x6, Pallas kernels, forward_step(): pl.pallas_call(forward_kernel, grid_spec=pltpu.PrefetchScalarGridSpec(num...  58.4 us
    pallas_call x1, Pallas kernels, body(): pl.pallas_call(queries_kernel, grid_spec=pltpu.PrefetchScalarGridSpec(num...  39.4 us
    ppermute x12, waiting for transfers between devices, group_sum(): gathered.append(lax.ppermute(value, axis, pairs(shift)))  32.2 us
    unnamed x175, local copies, waits for them, and re-layouts  23.5 us
    ppermute x6, starting transfers between devices, arrivals(): other = lax.ppermute(held, 'blk', between)  18.3 us
    ppermute x12, starting transfers between devices, group_sum(): gathered.append(lax.ppermute(value, axis, pairs(shift)))  17.8 us
    ppermute x6, waiting for transfers between devices, arrivals(): held = lax.ppermute(held, 'blk', onward)  17 us
  transfers between devices with their start and end apart: 42, of which 14 were waited for; matrix products, arithmetic and copies ran while one was open for 20% of the time, Pallas kernels for 37%

profile of v1, /device:TPU:0, one launch (start us, length us, event | category | flops | bytes accessed | tf_op | source)
XLA Modules:
  0.0 454.8 jit_solution(10448492415125985393)
XLA Ops:
  2.6 3.0 collective-permute-start
  9.7 3.4 collective-permute-done
  23.2 2.1 collective-permute-start.2
  26.1 12.1 %collective-permute-done.2.a_ref = bf16[1040,512]{1,0:T(8,128)(2,1)} collective-permute-done((bf16[1040,512]{1,0:T(8,128)(2,1)}, bf16[1040,512]{1,0:T(8,128)(2,1)}, u32[]{:S(2)}, u32[]{:S(2)}) %collective-permute-start.2) | collective-permute-done | bytes 1064992 | tf_op jit(solution)/shard_map/ppermute | solution.py:724
  38.2 2.5 collective-permute-start.3
  53.7 2.3 collective-permute-start.4
  56.6 16.0 %attend_own.1 = (bf16[5120,1152]{1,0:T(8,128)(2,1)}, f32[5,8,1024]{2,1,0:T(8,128)}, bf16[6,512,128]{2,1,0:T(8,128)(2,1)}, f32[512,384]{1,0:T(8,128)}, f32[512,128]{1,0:T(8,128)}) custom-call(s32[8]{0:T(128)} %stack.224.sc_ref, f32[16]{0:T(128)} %copy-done.49, bf16[1040,512]{1,0:T(8,128)(2,1)} %constant_dynamic-update-slice_fusion.a_ref, ...), custom_call_target="tpu_custom_call" | custom-call | flops 3221225472 | bytes 8388608 | tf_op jit(solution)/shard_map/attend_own/pallas_call | solution.py:684
  72.6 1.9 and_select_fusion.gen_in
  74.5 5.3 %attend_other.6 = (bf16[5120,1152]{1,0:T(8,128)(2,1)}, f32[5,8,1024]{2,1,0:T(8,128)}, f32[512,384]{1,0:T(8,128)}, f32[512,128]{1,0:T(8,128)}) custom-call(s32[8]{0:T(128)} %stack.250.sc_ref, f32[16]{0:T(128)} %copy-done.49, bf16[1040,512]{1,0:T(8,128)(2,1)} %collective-permute-done.2.a_ref, ...), custom_call_target="tpu_custom_call", output_to_operand_aliasing={{0}: (9, {}), {1}: (10, {}), {2}: (7, {}), {3}: (8, {})} | custom-call | flops 3221225472 | bytes 8388608 | tf_op jit(solution)/shard_map/attend_other/pallas_call | solution.py:703
  80.4 10.1 %collective-permute-start.5 = (bf16[1040,512]{1,0:T(8,128)(2,1)S(1)}, bf16[1040,512]{1,0:T(8,128)(2,1)S(1)}, u32[]{:S(2)}, u32[]{:S(2)}) collective-permute-start(bf16[1040,512]{1,0:T(8,128)(2,1)S(1)} %collective-permute-done.4.a_ref), channel_id=1, source_target_pairs={{0,2},{2,0},{4,6},{6,4},{8,10},{10,8},{12,14},{14,12},{16,18},{18,... | collective-permute-start | bytes 3194888 | tf_op jit(solution)/shard_map/ppermute | solution.py:725
  91.5 14.4 %attend_other.7 = (bf16[5120,1152]{1,0:T(8,128)(2,1)}, f32[5,8,1024]{2,1,0:T(8,128)}, f32[512,384]{1,0:T(8,128)}, f32[512,128]{1,0:T(8,128)}) custom-call(s32[8]{0:T(128)} %stack.245.sc_ref, f32[16]{0:T(128)} %copy-done.49, bf16[1040,512]{1,0:T(8,128)(2,1)} %copy-done.27, ...), custom_call_target="tpu_custom_call", output_to_operand_aliasing={{0}: (9, {}), {1}: (10, {}), {2}: (7, {}), {3}: (8, {})} | custom-call | flops 3221225472 | bytes 8388608 | tf_op jit(solution)/shard_map/attend_other/pallas_call | solution.py:703
  106.0 4.8 %attend_other.8 = (bf16[5120,1152]{1,0:T(8,128)(2,1)}, f32[5,8,1024]{2,1,0:T(8,128)}, f32[512,384]{1,0:T(8,128)}, f32[512,128]{1,0:T(8,128)}) custom-call(s32[8]{0:T(128)} %stack.240.sc_ref, f32[16]{0:T(128)} %copy-done.49, bf16[1040,512]{1,0:T(8,128)(2,1)} %collective-permute-done.3.a_ref, ...), custom_call_target="tpu_custom_call", output_to_operand_aliasing={{0}: (9, {}), {1}: (10, {}), {2}: (7, {}), {3}: (8, {})} | custom-call | flops 3221225472 | bytes 8388608 | tf_op jit(solution)/shard_map/attend_other/pallas_call | solution.py:703
  111.8 14.6 %attend_other.9 = (bf16[5120,1152]{1,0:T(8,128)(2,1)}, f32[5,8,1024]{2,1,0:T(8,128)}, f32[512,384]{1,0:T(8,128)}, f32[512,128]{1,0:T(8,128)}) custom-call(s32[8]{0:T(128)} %stack.235.sc_ref, f32[16]{0:T(128)} %copy-done.49, bf16[1040,512]{1,0:T(8,128)(2,1)} %copy-done.26, ...), custom_call_target="tpu_custom_call", output_to_operand_aliasing={{0}: (9, {}), {1}: (10, {}), {2}: (7, {}), {3}: (8, {})} | custom-call | flops 3221225472 | bytes 8388608 | tf_op jit(solution)/shard_map/attend_other/pallas_call | solution.py:703
  126.5 4.8 %attend_other.10 = (bf16[5120,1152]{1,0:T(8,128)(2,1)}, f32[5,8,1024]{2,1,0:T(8,128)}, f32[512,384]{1,0:T(8,128)}, f32[512,128]{1,0:T(8,128)}) custom-call(s32[8]{0:T(128)} %stack.230.sc_ref, f32[16]{0:T(128)} %copy-done.49, bf16[1040,512]{1,0:T(8,128)(2,1)} %copy-done.24, ...), custom_call_target="tpu_custom_call", output_to_operand_aliasing={{0}: (9, {}), {1}: (10, {}), {2}: (7, {}), {3}: (8, {})} | custom-call | flops 3221225472 | bytes 8388608 | tf_op jit(solution)/shard_map/attend_other/pallas_call | solution.py:703
  132.2 14.5 %attend_other.11 = (bf16[5120,1152]{1,0:T(8,128)(2,1)}, f32[5,8,1024]{2,1,0:T(8,128)}, f32[512,384]{1,0:T(8,128)}, f32[512,128]{1,0:T(8,128)}) custom-call(s32[8]{0:T(128)} %stack.222.sc_ref, f32[16]{0:T(128)} %copy-done.49, bf16[1040,512]{1,0:T(8,128)(2,1)} %copy-done.25, ...), custom_call_target="tpu_custom_call", output_to_operand_aliasing={{0}: (9, {}), {1}: (10, {}), {2}: (7, {}), {3}: (8, {})} | custom-call | flops 3221225472 | bytes 8388608 | tf_op jit(solution)/shard_map/attend_other/pallas_call | solution.py:703
  146.8 2.7 broadcast_select_fusion.17
  152.1 1.8 multiply_reduce_fusion.2
  156.4 3.4 multiply_convert_fusion
  167.8 2.3 copy.114
  177.0 2.4 pad_dynamic-slice_fusion
  185.6 2.0 scatter.41.ld_ref
  187.6 39.4 %grad_queries.1 = (bf16[512,384]{1,0:T(8,128)(2,1)}, f32[8,512]{1,0:T(8,128)}, f32[6,8,128]{2,1,0:T(8,128)}) custom-call(s32[8]{0:T(128)} %stack.224.sc_ref, f32[16]{0:T(128)} %copy-done.49, bf16[5120,1152]{1,0:T(8,128)(2,1)} %get-tuple-element.227.qkv_ref.q_ref.kv0_ref.kv1_ref, f32[5,8,1024]{2,1,0:T(8,128)} %get-tuple-element.228.mask_ref, ...), custom_call_target="tpu_custom_call" | custom-call | flops 19327352832 | bytes 8388608 | tf_op jit(solution)/shard_map/grad_queries/pallas_call | solution.py:822
  240.6 2.2 concatenate.147
  247.0 2.0 fusion.15
  260.2 4.9 %collective-permute-done.11.dox_ref = bf16[1024,512]{1,0:T(8,128)(2,1)} collective-permute-done((bf16[1024,512]{1,0:T(8,128)(2,1)S(1)}, bf16[1024,512]{1,0:T(8,128)(2,1)}, u32[]{:S(2)}, u32[]{:S(2)}) %collective-permute-start.11) | collective-permute-done | bytes 1048608 | tf_op jit(solution)/shard_map/ppermute | solution.py:724
  267.7 2.9 add_convert_fusion
  272.6 20.4 %grad_keys_own.1.dkv_in = f32[512,768]{1,0:T(8,128)} custom-call(s32[8]{0:T(128)} %constant_dynamic-update-slice_fusion.11.sc_ref, f32[16]{0:T(128)} %copy-done.49, f32[48]{0:T(128)} %pad_maximum_fusion.20.pieces_ref, bf16[1024,512]{1,0:T(8,128)(2,1)} %copy-done.14, ...), custom_call_target="tpu_custom_call", output_to_operand_aliasing={{}: (10, {})} | custom-call | flops 6442450944 | bytes 8388608 | tf_op jit(solution)/shard_map/grad_keys_own/pallas_call | solution.py:870
  293.0 4.3 grad_keys_other.6.dkv_in
  297.3 6.8 %collective-permute-start.15 = (bf16[1024,512]{1,0:T(8,128)(2,1)S(1)}, bf16[1024,512]{1,0:T(8,128)(2,1)}, u32[]{:S(2)}, u32[]{:S(2)}) collective-permute-start(bf16[1024,512]{1,0:T(8,128)(2,1)S(1)} %collective-permute-done.12.dox_ref), channel_id=1, source_target_pairs={{0,2},{2,0},{4,6},{6,4},{8,10},{10,8},{12,14},{14,12},{16,18},{18,... | collective-permute-start | bytes 3145736 | tf_op jit(solution)/shard_map/ppermute | solution.py:725
  307.4 12.3 %grad_keys_other.7.dkv_in = f32[512,768]{1,0:T(8,128)} custom-call(s32[8]{0:T(128)} %copy-done.68, f32[16]{0:T(128)} %copy-done.49, f32[48]{0:T(128)} %pad_maximum_fusion.20.pieces_ref, bf16[1024,512]{1,0:T(8,128)(2,1)} %collective-permute-done.16.dox_ref, ...), custom_call_target="tpu_custom_call", output_to_operand_aliasing={{}: (10, {})} | custom-call | flops 6442450944 | bytes 8388608 | tf_op jit(solution)/shard_map/grad_keys_other/pallas_call | solution.py:870
  319.8 2.6 collective-permute-start.33
  322.5 2.8 collective-permute-start.35
  325.3 4.3 grad_keys_other.8.dkv_in
  329.6 2.0 collective-permute-done.34
  332.4 2.9 collective-permute-start.36
  335.3 4.9 %collective-permute-start.37 = (bf16[112,512]{1,0:T(8,128)(2,1)}, bf16[112,512]{1,0:T(8,128)(2,1)}, u32[]{:S(2)}, u32[]{:S(2)}) collective-permute-start(bf16[112,512]{1,0:T(8,128)(2,1)} %get-tuple-element.293), channel_id=1, source_target_pairs={{0,16},{2,18},{4,20},{6,22},{8,24},{10,26},{12,28},{14,30},{16,0},... | collective-permute-start | bytes 344072 | tf_op jit(solution)/shard_map/ppermute | solution.py:509
  341.5 12.1 %grad_keys_other.9.dkv_in = f32[512,768]{1,0:T(8,128)} custom-call(s32[8]{0:T(128)} %copy-done.64, f32[16]{0:T(128)} %copy-done.49, f32[48]{0:T(128)} %pad_maximum_fusion.20.pieces_ref, bf16[1024,512]{1,0:T(8,128)(2,1)} %collective-permute-done.15.dox_ref, ...), custom_call_target="tpu_custom_call", output_to_operand_aliasing={{}: (10, {})} | custom-call | flops 6442450944 | bytes 8388608 | tf_op jit(solution)/shard_map/grad_keys_other/pallas_call | solution.py:870
  353.6 4.5 grad_keys_other.10.dkv_in
  359.1 12.1 %grad_keys_other.11 = f32[512,768]{1,0:T(8,128)} custom-call(s32[8]{0:T(128)} %constant_dynamic-update-slice_fusion.17.sc_ref, f32[16]{0:T(128)} %copy-done.49, f32[48]{0:T(128)} %pad_maximum_fusion.20.pieces_ref, bf16[1024,512]{1,0:T(8,128)(2,1)} %copy-done.30, ...), custom_call_target="tpu_custom_call", output_to_operand_aliasing={{}: (10, {})} | custom-call | flops 6442450944 | bytes 8388608 | tf_op jit(solution)/shard_map/grad_keys_other/pallas_call | solution.py:870
  384.4 9.8 %collective-permute-done.39 = bf16[448,512]{1,0:T(8,128)(2,1)S(1)} collective-permute-done((bf16[448,512]{1,0:T(8,128)(2,1)S(1)}, bf16[448,512]{1,0:T(8,128)(2,1)S(1)}, u32[]{:S(2)}, u32[]{:S(2)}) %collective-permute-start.39) | collective-permute-done | bytes 458784 | tf_op jit(solution)/shard_map/ppermute | solution.py:509
  396.6 5.2 %collective-permute-done.20 = bf16[224,384]{1,0:T(8,128)(2,1)S(1)} collective-permute-done((bf16[224,384]{1,0:T(8,128)(2,1)S(1)}, bf16[224,384]{1,0:T(8,128)(2,1)S(1)}, u32[]{:S(2)}, u32[]{:S(2)}) %collective-permute-start.20) | collective-permute-done | bytes 172064 | tf_op jit(solution)/shard_map/ppermute | solution.py:504
  402.4 3.3 collective-permute-start.23
  405.8 10.6 %collective-permute-done.40 = bf16[896,512]{1,0:T(8,128)(2,1)S(1)} collective-permute-done((bf16[896,512]{1,0:T(8,128)(2,1)S(1)}, bf16[896,512]{1,0:T(8,128)(2,1)S(1)}, u32[]{:S(2)}, u32[]{:S(2)}) %collective-permute-start.40) | collective-permute-done | bytes 917536 | tf_op jit(solution)/shard_map/ppermute | solution.py:509
  417.4 3.9 collective-permute-start.26
  421.3 1.8 collective-permute-done.24
  426.4 3.7 collective-permute-done.27
  434.4 5.7 %collective-permute-done.28 = bf16[448,384]{1,0:T(8,128)(2,1)S(1)} collective-permute-done((bf16[448,384]{1,0:T(8,128)(2,1)S(1)}, bf16[448,384]{1,0:T(8,128)(2,1)S(1)}, u32[]{:S(2)}, u32[]{:S(2)}) %collective-permute-start.28) | collective-permute-done | bytes 344096 | tf_op jit(solution)/shard_map/ppermute | solution.py:509
  451.3 3.1 fusion.87
  (435 shorter events, 135.3 us)
Async XLA Ops:
  0.6 155.4 %copy-start = (bf16[1024,512]{1,0:T(8,128)(2,1)S(1)}, bf16[1024,512]{1,0:T(8,128)(2,1)}, u32[]{:S(2)}) copy-start(bf16[1024,512]{1,0:T(8,128)(2,1)} %param.53) | copy-start | bytes 3145732
  2.6 10.5 %collective-permute-start = (bf16[272,512]{1,0:T(8,128)(2,1)S(1)}, bf16[272,512]{1,0:T(8,128)(2,1)S(1)}, u32[]{:S(2)}, u32[]{:S(2)}) collective-permute-start(bf16[272,512]{1,0:T(8,128)(2,1)S(1)} %dynamic-slice_bitcast_fusion), channel_id=1, source_target_pairs={{0,4},{2,6},{4,0},{6,2},{8,12},{10,14},{12,8},{14,10},{16,20},{18,... | collective-permute-start | bytes 835592 | tf_op jit(solution)/shard_map/ppermute | solution.py:567
  7.3 42.8 %collective-permute-start.9 = (bf16[256,512]{1,0:T(8,128)(2,1)}, bf16[256,512]{1,0:T(8,128)(2,1)}, u32[]{:S(2)}, u32[]{:S(2)}) collective-permute-start(bf16[256,512]{1,0:T(8,128)(2,1)} %dynamic-slice_bitcast_fusion.2), channel_id=1, source_target_pairs={{0,4},{2,6},{4,0},{6,2},{8,12},{10,14},{12,8},{14,10},{16,20},{18,... | collective-permute-start | bytes 786440 | tf_op jit(solution)/shard_map/ppermute | solution.py:567
  13.2 138.9 %copy-start.7 = (bf16[256,512]{1,0:T(8,128)(2,1)}, bf16[256,512]{1,0:T(8,128)(2,1)S(1)}, u32[]{:S(2)}) copy-start(bf16[256,512]{1,0:T(8,128)(2,1)S(1)} %slice.413) | copy-start | bytes 786436
  14.3 2.0 collective-permute-start.1
  16.5 33.5 %copy-start.40 = (bf16[2,256,512]{2,1,0:T(8,128)(2,1)S(1)}, bf16[2,256,512]{2,1,0:T(8,128)(2,1)}, u32[]{:S(2)}) copy-start(bf16[2,256,512]{2,1,0:T(8,128)(2,1)} %param.43) | copy-start | bytes 1572868
  23.2 15.0 %collective-permute-start.2 = (bf16[1040,512]{1,0:T(8,128)(2,1)}, bf16[1040,512]{1,0:T(8,128)(2,1)}, u32[]{:S(2)}, u32[]{:S(2)}) collective-permute-start(bf16[1040,512]{1,0:T(8,128)(2,1)} %constant_dynamic-update-slice_fusion.a_ref), channel_id=1, source_target_pairs={{0,8},{2,0},{4,12},{6,4},{8,16},{10,2},{12,20},{14,6},{16,24},{18,... | collective-permute-start | bytes 3194888 | tf_op jit(solution)/shard_map/ppermute | solution.py:724
  25.5 31.2 %copy-start.2 = (bf16[512,1152]{1,0:T(8,128)(2,1)}, bf16[512,1152]{1,0:T(8,128)(2,1)S(1)}, u32[]{:S(2)}) copy-start(bf16[512,1152]{1,0:T(8,128)(2,1)S(1)} %constant_dynamic-update-slice_fusion.1.w_ref) | copy-start | bytes 3538948
  38.2 15.5 %collective-permute-start.3 = (bf16[1040,512]{1,0:T(8,128)(2,1)}, bf16[1040,512]{1,0:T(8,128)(2,1)}, u32[]{:S(2)}, u32[]{:S(2)}) collective-permute-start(bf16[1040,512]{1,0:T(8,128)(2,1)} %collective-permute-done.2.a_ref), channel_id=1, source_target_pairs={{0,8},{2,0},{4,12},{6,4},{8,16},{10,2},{12,20},{14,6},{16,24},{18,... | collective-permute-start | bytes 3194888 | tf_op jit(solution)/shard_map/ppermute | solution.py:724
  53.7 36.9 %collective-permute-start.7 = (bf16[1040,512]{1,0:T(8,128)(2,1)}, bf16[1040,512]{1,0:T(8,128)(2,1)S(1)}, u32[]{:S(2)}, u32[]{:S(2)}) collective-permute-start(bf16[1040,512]{1,0:T(8,128)(2,1)} %collective-permute-done.2.a_ref), channel_id=1, source_target_pairs={{0,2},{2,0},{4,6},{6,4},{8,10},{10,8},{12,14},{14,12},{16,18},{18,... | collective-permute-start | bytes 3194888 | tf_op jit(solution)/shard_map/ppermute | solution.py:725
  53.7 26.7 %collective-permute-start.4 = (bf16[1040,512]{1,0:T(8,128)(2,1)}, bf16[1040,512]{1,0:T(8,128)(2,1)S(1)}, u32[]{:S(2)}, u32[]{:S(2)}) collective-permute-start(bf16[1040,512]{1,0:T(8,128)(2,1)} %collective-permute-done.3.a_ref), channel_id=1, source_target_pairs={{0,8},{2,0},{4,12},{6,4},{8,16},{10,2},{12,20},{14,6},{16,24},{18,... | collective-permute-start | bytes 3194888 | tf_op jit(solution)/shard_map/ppermute | solution.py:724
  72.6 38.2 %collective-permute-start.6 = (bf16[1040,512]{1,0:T(8,128)(2,1)}, bf16[1040,512]{1,0:T(8,128)(2,1)S(1)}, u32[]{:S(2)}, u32[]{:S(2)}) collective-permute-start(bf16[1040,512]{1,0:T(8,128)(2,1)} %collective-permute-done.3.a_ref), channel_id=1, source_target_pairs={{0,2},{2,0},{4,6},{6,4},{8,10},{10,8},{12,14},{14,12},{16,18},{18,... | collective-permute-start | bytes 3194888 | tf_op jit(solution)/shard_map/ppermute | solution.py:725
  80.4 25.5 %copy-start.24 = (bf16[1040,512]{1,0:T(8,128)(2,1)}, bf16[1040,512]{1,0:T(8,128)(2,1)S(1)}, u32[]{:S(2)}) copy-start(bf16[1040,512]{1,0:T(8,128)(2,1)S(1)} %collective-permute-done.4.a_ref) | copy-start | bytes 3194884
  80.4 50.8 %collective-permute-start.5 = (bf16[1040,512]{1,0:T(8,128)(2,1)S(1)}, bf16[1040,512]{1,0:T(8,128)(2,1)S(1)}, u32[]{:S(2)}, u32[]{:S(2)}) collective-permute-start(bf16[1040,512]{1,0:T(8,128)(2,1)S(1)} %collective-permute-done.4.a_ref), channel_id=1, source_target_pairs={{0,2},{2,0},{4,6},{6,4},{8,10},{10,8},{12,14},{14,12},{16,18},{18,... | collective-permute-start | bytes 3194888 | tf_op jit(solution)/shard_map/ppermute | solution.py:725
  179.4 88.3 %collective-permute-start.30 = (bf16[1792,512]{1,0:T(8,128)(2,1)}, bf16[1792,512]{1,0:T(8,128)(2,1)}, u32[]{:S(2)}, u32[]{:S(2)}) collective-permute-start(bf16[1792,512]{1,0:T(8,128)(2,1)} %pad_dynamic-slice_fusion), channel_id=1, source_target_pairs={{0,2},{2,0},{4,6},{6,4},{8,10},{10,8},{12,14},{14,12},{16,18},{18,... | collective-permute-start | bytes 5505032 | tf_op jit(solution)/shard_map/ppermute | solution.py:504
  187.6 47.3 %copy-start.50 = (f32[512,6]{0,1:T(8,128)S(1)}, f32[512,6]{0,1:T(8,128)}, u32[]{:S(2)}) copy-start(f32[512,6]{0,1:T(8,128)} %neg.25) | copy-start | bytes 36868
  244.5 6.8 %collective-permute-start.10 = (bf16[512,512]{1,0:T(8,128)(2,1)}, bf16[512,512]{1,0:T(8,128)(2,1)}, u32[]{:S(2)}, u32[]{:S(2)}) collective-permute-start(bf16[512,512]{1,0:T(8,128)(2,1)} %fusion.32), channel_id=1, source_target_pairs={{0,2},{2,0},{4,6},{6,4},{8,10},{10,8},{12,14},{14,12},{16,18},{18,... | collective-permute-start | bytes 1572872 | tf_op jit(solution)/shard_map/ppermute | solution.py:578
  249.8 8.7 %collective-permute-start.8 = (bf16[256,512]{1,0:T(8,128)(2,1)}, bf16[256,512]{1,0:T(8,128)(2,1)}, u32[]{:S(2)}, u32[]{:S(2)}) collective-permute-start(bf16[256,512]{1,0:T(8,128)(2,1)} %dynamic-slice_bitcast_fusion.3), channel_id=1, source_target_pairs={{0,4},{2,6},{4,0},{6,2},{8,12},{10,14},{12,8},{14,10},{16,20},{18,... | collective-permute-start | bytes 786440 | tf_op jit(solution)/shard_map/ppermute | solution.py:574
  252.8 12.3 %collective-permute-start.11 = (bf16[1024,512]{1,0:T(8,128)(2,1)S(1)}, bf16[1024,512]{1,0:T(8,128)(2,1)}, u32[]{:S(2)}, u32[]{:S(2)}) collective-permute-start(bf16[1024,512]{1,0:T(8,128)(2,1)S(1)} %pad_maximum_fusion.4.dox_ref), channel_id=1, source_target_pairs={{0,8},{2,0},{4,12},{6,4},{8,16},{10,2},{12,20},{14,6},{16,24},{18,... | collective-permute-start | bytes 3145736 | tf_op jit(solution)/shard_map/ppermute | solution.py:724
  265.1 42.3 %collective-permute-start.16 = (bf16[1024,512]{1,0:T(8,128)(2,1)}, bf16[1024,512]{1,0:T(8,128)(2,1)}, u32[]{:S(2)}, u32[]{:S(2)}) collective-permute-start(bf16[1024,512]{1,0:T(8,128)(2,1)} %collective-permute-done.11.dox_ref), channel_id=1, source_target_pairs={{0,2},{2,0},{4,6},{6,4},{8,10},{10,8},{12,14},{14,12},{16,18},{18,... | collective-permute-start | bytes 3145736 | tf_op jit(solution)/shard_map/ppermute | solution.py:725
  266.5 30.8 %collective-permute-start.12 = (bf16[1024,512]{1,0:T(8,128)(2,1)}, bf16[1024,512]{1,0:T(8,128)(2,1)S(1)}, u32[]{:S(2)}, u32[]{:S(2)}) collective-permute-start(bf16[1024,512]{1,0:T(8,128)(2,1)} %collective-permute-done.11.dox_ref), channel_id=1, source_target_pairs={{0,8},{2,0},{4,12},{6,4},{8,16},{10,2},{12,20},{14,6},{16,24},{18,... | collective-permute-start | bytes 3145736 | tf_op jit(solution)/shard_map/ppermute | solution.py:724
  270.7 34.8 %collective-permute-start.31 = (bf16[896,512]{1,0:T(8,128)(2,1)S(1)}, bf16[896,512]{1,0:T(8,128)(2,1)S(1)}, u32[]{:S(2)}, u32[]{:S(2)}) collective-permute-start(bf16[896,512]{1,0:T(8,128)(2,1)S(1)} %constant_dynamic-slice_fusion.4), channel_id=1, source_target_pairs={{0,4},{2,6},{4,0},{6,2},{8,12},{10,14},{12,8},{14,10},{16,20},{18,... | collective-permute-start | bytes 2752520 | tf_op jit(solution)/shard_map/ppermute | solution.py:504
  297.3 44.3 %collective-permute-start.15 = (bf16[1024,512]{1,0:T(8,128)(2,1)S(1)}, bf16[1024,512]{1,0:T(8,128)(2,1)}, u32[]{:S(2)}, u32[]{:S(2)}) collective-permute-start(bf16[1024,512]{1,0:T(8,128)(2,1)S(1)} %collective-permute-done.12.dox_ref), channel_id=1, source_target_pairs={{0,2},{2,0},{4,6},{6,4},{8,10},{10,8},{12,14},{14,12},{16,18},{18,... | collective-permute-start | bytes 3145736 | tf_op jit(solution)/shard_map/ppermute | solution.py:725
  304.1 37.5 %collective-permute-start.13 = (bf16[1024,512]{1,0:T(8,128)(2,1)S(1)}, bf16[1024,512]{1,0:T(8,128)(2,1)}, u32[]{:S(2)}, u32[]{:S(2)}) collective-permute-start(bf16[1024,512]{1,0:T(8,128)(2,1)S(1)} %collective-permute-done.12.dox_ref), channel_id=1, source_target_pairs={{0,8},{2,0},{4,12},{6,4},{8,16},{10,2},{12,20},{14,6},{16,24},{18,... | collective-permute-start | bytes 3145736 | tf_op jit(solution)/shard_map/ppermute | solution.py:724
  305.8 13.9 %collective-permute-start.32 = (bf16[448,512]{1,0:T(8,128)(2,1)S(1)}, bf16[448,512]{1,0:T(8,128)(2,1)S(1)}, u32[]{:S(2)}, u32[]{:S(2)}) collective-permute-start(bf16[448,512]{1,0:T(8,128)(2,1)S(1)} %constant_dynamic-slice_fusion.3), channel_id=1, source_target_pairs={{0,1},{1,0},{2,3},{3,2},{4,5},{5,4},{6,7},{7,6},{8,9},{9,8},{10,11... | collective-permute-start | bytes 1376264 | tf_op jit(solution)/shard_map/ppermute | solution.py:504
  319.8 9.8 %collective-permute-start.33 = (bf16[112,512]{1,0:T(8,128)(2,1)S(1)}, bf16[112,512]{1,0:T(8,128)(2,1)S(1)}, u32[]{:S(2)}, u32[]{:S(2)}) collective-permute-start(bf16[112,512]{1,0:T(8,128)(2,1)S(1)} %get-tuple-element.340), channel_id=1, source_target_pairs={{0,8},{2,10},{4,12},{6,14},{8,16},{10,18},{12,20},{14,22},{16,24},... | collective-permute-start | bytes 344072 | tf_op jit(solution)/shard_map/ppermute | solution.py:504
  322.5 9.2 %collective-permute-start.34 = (bf16[112,512]{1,0:T(8,128)(2,1)S(1)}, bf16[112,512]{1,0:T(8,128)(2,1)S(1)}, u32[]{:S(2)}, u32[]{:S(2)}) collective-permute-start(bf16[112,512]{1,0:T(8,128)(2,1)S(1)} %get-tuple-element.342), channel_id=1, source_target_pairs={{0,16},{2,18},{4,20},{6,22},{8,24},{10,26},{12,28},{14,30},{16,0},... | collective-permute-start | bytes 344072 | tf_op jit(solution)/shard_map/ppermute | solution.py:504
  322.5 9.2 %collective-permute-start.35 = (bf16[112,512]{1,0:T(8,128)(2,1)S(1)}, bf16[112,512]{1,0:T(8,128)(2,1)S(1)}, u32[]{:S(2)}, u32[]{:S(2)}) collective-permute-start(bf16[112,512]{1,0:T(8,128)(2,1)S(1)} %get-tuple-element.341), channel_id=1, source_target_pairs={{0,24},{2,26},{4,28},{6,30},{8,0},{10,2},{12,4},{14,6},{16,8},{18,... | collective-permute-start | bytes 344072 | tf_op jit(solution)/shard_map/ppermute | solution.py:504
  332.4 46.9 %collective-permute-start.36 = (bf16[112,512]{1,0:T(8,128)(2,1)}, bf16[112,512]{1,0:T(8,128)(2,1)}, u32[]{:S(2)}, u32[]{:S(2)}) collective-permute-start(bf16[112,512]{1,0:T(8,128)(2,1)} %get-tuple-element.293), channel_id=1, source_target_pairs={{0,8},{2,10},{4,12},{6,14},{8,16},{10,18},{12,20},{14,22},{16,24},... | collective-permute-start | bytes 344072 | tf_op jit(solution)/shard_map/ppermute | solution.py:509
  335.3 44.9 %collective-permute-start.37 = (bf16[112,512]{1,0:T(8,128)(2,1)}, bf16[112,512]{1,0:T(8,128)(2,1)}, u32[]{:S(2)}, u32[]{:S(2)}) collective-permute-start(bf16[112,512]{1,0:T(8,128)(2,1)} %get-tuple-element.293), channel_id=1, source_target_pairs={{0,16},{2,18},{4,20},{6,22},{8,24},{10,26},{12,28},{14,30},{16,0},... | collective-permute-start | bytes 344072 | tf_op jit(solution)/shard_map/ppermute | solution.py:509
  340.3 40.9 %collective-permute-start.38 = (bf16[112,512]{1,0:T(8,128)(2,1)}, bf16[112,512]{1,0:T(8,128)(2,1)S(1)}, u32[]{:S(2)}, u32[]{:S(2)}) collective-permute-start(bf16[112,512]{1,0:T(8,128)(2,1)} %get-tuple-element.293), channel_id=1, source_target_pairs={{0,24},{2,26},{4,28},{6,30},{8,0},{10,2},{12,4},{14,6},{16,8},{18,... | collective-permute-start | bytes 344072 | tf_op jit(solution)/shard_map/ppermute | solution.py:509
  341.5 16.6 %collective-permute-start.14 = (bf16[1024,512]{1,0:T(8,128)(2,1)}, bf16[1024,512]{1,0:T(8,128)(2,1)S(1)}, u32[]{:S(2)}, u32[]{:S(2)}) collective-permute-start(bf16[1024,512]{1,0:T(8,128)(2,1)} %collective-permute-done.13.dox_ref), channel_id=1, source_target_pairs={{0,2},{2,0},{4,6},{6,4},{8,10},{10,8},{12,14},{14,12},{16,18},{18,... | collective-permute-start | bytes 3145736 | tf_op jit(solution)/shard_map/ppermute | solution.py:725
  379.2 3.4 collective-permute-start.18
  381.2 13.0 %collective-permute-start.39 = (bf16[448,512]{1,0:T(8,128)(2,1)S(1)}, bf16[448,512]{1,0:T(8,128)(2,1)S(1)}, u32[]{:S(2)}, u32[]{:S(2)}) collective-permute-start(bf16[448,512]{1,0:T(8,128)(2,1)S(1)} %bitcast.164), channel_id=1, source_target_pairs={{0,1},{1,0},{2,3},{3,2},{4,5},{5,4},{6,7},{7,6},{8,9},{9,8},{10,11... | collective-permute-start | bytes 1376264 | tf_op jit(solution)/shard_map/ppermute | solution.py:509
  382.9 13.0 %collective-permute-start.19 = (bf16[448,384]{1,0:T(8,128)(2,1)S(1)}, bf16[448,384]{1,0:T(8,128)(2,1)S(1)}, u32[]{:S(2)}, u32[]{:S(2)}) collective-permute-start(bf16[448,384]{1,0:T(8,128)(2,1)S(1)} %constant_dynamic-slice_fusion.9), channel_id=1, source_target_pairs={{0,4},{2,6},{4,0},{6,2},{8,12},{10,14},{12,8},{14,10},{16,20},{18,... | collective-permute-start | bytes 1032200 | tf_op jit(solution)/shard_map/ppermute | solution.py:504
  394.3 22.0 %collective-permute-start.40 = (bf16[896,512]{1,0:T(8,128)(2,1)S(1)}, bf16[896,512]{1,0:T(8,128)(2,1)S(1)}, u32[]{:S(2)}, u32[]{:S(2)}) collective-permute-start(bf16[896,512]{1,0:T(8,128)(2,1)S(1)} %pad_maximum_fusion.5), channel_id=1, source_target_pairs={{0,4},{2,6},{4,0},{6,2},{8,12},{10,14},{12,8},{14,10},{16,20},{18,... | collective-permute-start | bytes 2752520 | tf_op jit(solution)/shard_map/ppermute | solution.py:509
  396.0 5.8 %collective-permute-start.20 = (bf16[224,384]{1,0:T(8,128)(2,1)S(1)}, bf16[224,384]{1,0:T(8,128)(2,1)S(1)}, u32[]{:S(2)}, u32[]{:S(2)}) collective-permute-start(bf16[224,384]{1,0:T(8,128)(2,1)S(1)} %constant_dynamic-slice_fusion.8), channel_id=1, source_target_pairs={{0,1},{1,0},{2,3},{3,2},{4,5},{5,4},{6,7},{7,6},{8,9},{9,8},{10,11... | collective-permute-start | bytes 516104 | tf_op jit(solution)/shard_map/ppermute | solution.py:504
  401.9 14.8 %collective-permute-start.21 = (bf16[56,384]{1,0:T(8,128)(2,1)S(1)}, bf16[56,384]{1,0:T(8,128)(2,1)S(1)}, u32[]{:S(2)}, u32[]{:S(2)}) collective-permute-start(bf16[56,384]{1,0:T(8,128)(2,1)S(1)} %get-tuple-element.356), channel_id=1, source_target_pairs={{0,8},{2,10},{4,12},{6,14},{8,16},{10,18},{12,20},{14,22},{16,24},... | collective-permute-start | bytes 129032 | tf_op jit(solution)/shard_map/ppermute | solution.py:504
  401.9 14.8 %collective-permute-start.22 = (bf16[56,384]{1,0:T(8,128)(2,1)S(1)}, bf16[56,384]{1,0:T(8,128)(2,1)S(1)}, u32[]{:S(2)}, u32[]{:S(2)}) collective-permute-start(bf16[56,384]{1,0:T(8,128)(2,1)S(1)} %get-tuple-element.358), channel_id=1, source_target_pairs={{0,16},{2,18},{4,20},{6,22},{8,24},{10,26},{12,28},{14,30},{16,0},... | collective-permute-start | bytes 129032 | tf_op jit(solution)/shard_map/ppermute | solution.py:504
  402.4 14.3 %collective-permute-start.23 = (bf16[56,384]{1,0:T(8,128)(2,1)S(1)}, bf16[56,384]{1,0:T(8,128)(2,1)S(1)}, u32[]{:S(2)}, u32[]{:S(2)}) collective-permute-start(bf16[56,384]{1,0:T(8,128)(2,1)S(1)} %get-tuple-element.357), channel_id=1, source_target_pairs={{0,24},{2,26},{4,28},{6,30},{8,0},{10,2},{12,4},{14,6},{16,8},{18,... | collective-permute-start | bytes 129032 | tf_op jit(solution)/shard_map/ppermute | solution.py:504
  416.8 6.3 %collective-permute-start.24 = (bf16[56,384]{1,0:T(8,128)(2,1)S(1)}, bf16[56,384]{1,0:T(8,128)(2,1)S(1)}, u32[]{:S(2)}, u32[]{:S(2)}) collective-permute-start(bf16[56,384]{1,0:T(8,128)(2,1)S(1)} %get-tuple-element.295), channel_id=1, source_target_pairs={{0,8},{2,10},{4,12},{6,14},{8,16},{10,18},{12,20},{14,22},{16,24},... | collective-permute-start | bytes 129032 | tf_op jit(solution)/shard_map/ppermute | solution.py:509
  417.0 23.3 %collective-permute-start.41 = (bf16[1792,512]{1,0:T(8,128)(2,1)S(1)}, bf16[1792,512]{1,0:T(8,128)(2,1)S(1)}, u32[]{:S(2)}, u32[]{:S(2)}) collective-permute-start(bf16[1792,512]{1,0:T(8,128)(2,1)S(1)} %pad_maximum_fusion.2), channel_id=1, source_target_pairs={{0,2},{2,0},{4,6},{6,4},{8,10},{10,8},{12,14},{14,12},{16,18},{18,... | collective-permute-start | bytes 5505032 | tf_op jit(solution)/shard_map/ppermute | solution.py:509
  417.1 6.1 %collective-permute-start.25 = (bf16[56,384]{1,0:T(8,128)(2,1)S(1)}, bf16[56,384]{1,0:T(8,128)(2,1)S(1)}, u32[]{:S(2)}, u32[]{:S(2)}) collective-permute-start(bf16[56,384]{1,0:T(8,128)(2,1)S(1)} %get-tuple-element.295), channel_id=1, source_target_pairs={{0,16},{2,18},{4,20},{6,22},{8,24},{10,26},{12,28},{14,30},{16,0},... | collective-permute-start | bytes 129032 | tf_op jit(solution)/shard_map/ppermute | solution.py:509
  417.4 6.5 %collective-permute-start.26 = (bf16[56,384]{1,0:T(8,128)(2,1)S(1)}, bf16[56,384]{1,0:T(8,128)(2,1)S(1)}, u32[]{:S(2)}, u32[]{:S(2)}) collective-permute-start(bf16[56,384]{1,0:T(8,128)(2,1)S(1)} %get-tuple-element.295), channel_id=1, source_target_pairs={{0,24},{2,26},{4,28},{6,30},{8,0},{10,2},{12,4},{14,6},{16,8},{18,... | collective-permute-start | bytes 129032 | tf_op jit(solution)/shard_map/ppermute | solution.py:509
  423.9 6.2 %collective-permute-start.27 = (bf16[224,384]{1,0:T(8,128)(2,1)S(1)}, bf16[224,384]{1,0:T(8,128)(2,1)S(1)}, u32[]{:S(2)}, u32[]{:S(2)}) collective-permute-start(bf16[224,384]{1,0:T(8,128)(2,1)S(1)} %bitcast.165), channel_id=1, source_target_pairs={{0,1},{1,0},{2,3},{3,2},{4,5},{5,4},{6,7},{7,6},{8,9},{9,8},{10,11... | collective-permute-start | bytes 516104 | tf_op jit(solution)/shard_map/ppermute | solution.py:509
  424.8 8.6 %collective-permute-start.17 = (bf16[256,512]{1,0:T(8,128)(2,1)S(1)}, bf16[256,512]{1,0:T(8,128)(2,1)S(1)}, u32[]{:S(2)}, u32[]{:S(2)}) collective-permute-start(bf16[256,512]{1,0:T(8,128)(2,1)S(1)} %dynamic-slice_bitcast_fusion.1), channel_id=1, source_target_pairs={{0,4},{2,6},{4,0},{6,2},{8,12},{10,14},{12,8},{14,10},{16,20},{18,... | collective-permute-start | bytes 786440 | tf_op jit(solution)/shard_map/ppermute | solution.py:574
  430.2 9.9 %collective-permute-start.28 = (bf16[448,384]{1,0:T(8,128)(2,1)S(1)}, bf16[448,384]{1,0:T(8,128)(2,1)S(1)}, u32[]{:S(2)}, u32[]{:S(2)}) collective-permute-start(bf16[448,384]{1,0:T(8,128)(2,1)S(1)} %pad_maximum_fusion.11), channel_id=1, source_target_pairs={{0,4},{2,6},{4,0},{6,2},{8,12},{10,14},{12,8},{14,10},{16,20},{18,... | collective-permute-start | bytes 1032200 | tf_op jit(solution)/shard_map/ppermute | solution.py:509
  440.3 7.7 %collective-permute-start.29 = (bf16[896,384]{1,0:T(8,128)(2,1)S(1)}, bf16[896,384]{1,0:T(8,128)(2,1)S(1)}, u32[]{:S(2)}, u32[]{:S(2)}) collective-permute-start(bf16[896,384]{1,0:T(8,128)(2,1)S(1)} %pad_maximum_fusion.6), channel_id=1, source_target_pairs={{0,2},{2,0},{4,6},{6,4},{8,10},{10,8},{12,14},{14,12},{16,18},{18,... | collective-permute-start | bytes 2064392 | tf_op jit(solution)/shard_map/ppermute | solution.py:509
  (72 other events, 311.6 us)
